TPU v7x, 512 devices: a whole 4x8x8 slice. The times are simulated.
512 devices in a mesh: atom: 16 (over x, y_lo, core), row: 8 (over z), col: 4 (over y_hi).
Axes of the slice: x: 4, y: 8 (y_hi: 4, y_lo: 2; y = y_hi * 2 + y_lo), z: 8, core: 2. Of those that a mesh axis runs over, the one named last changes fastest.
Arguments:
- codes: bfloat16 [128, 64, 2048], P('row', 'col', 'atom'), may hold values from -1.5 to 1.5
- image: bfloat16 [128, 64, 128], P('row', 'col'), may hold values from -6 to 6
- master: float32 [128, 7, 7, 2048], P(('row', 'col'), None, None, 'atom'), may hold values from -0.078125 to 0.078125
- moment: float32 [128, 7, 7, 2048], P(('row', 'col'), None, None, 'atom'), may hold values from -120 to 120
- second: float32 [128, 7, 7, 2048], P(('row', 'col'), None, None, 'atom'), may hold values from 100 to 4000
Outputs:
- new_codes: bfloat16 [128, 64, 2048], P('row', 'col', 'atom')
- new_dictionary: float32 [128, 7, 7, 2048], P(('row', 'col'), None, None, 'atom')
- new_moment: float32 [128, 7, 7, 2048], P(('row', 'col'), None, None, 'atom')
- new_second: float32 [128, 7, 7, 2048], P(('row', 'col'), None, None, 'atom')
All inputs are finite; a program needn't handle non-finite values.
Results may differ from a plain program's by a relative error of at most 0.007.
Values may be sent and summed in bfloat16 or wider, within the bound.
A program may use at most 64 MiB of HBM per device.

v0:
```python
import jax
import jax.numpy as jnp
from jax import lax
from jax.sharding import PartitionSpec as P

first_fix = 0.9999734386011124
second_fix = 0.09520785288629038


def gather_axes(value, axes, dim):
    if not axes:
        return value
    nearer = lax.all_gather(value, axes[-1], axis=dim, tiled=True)
    return gather_axes(nearer, axes[:-1], dim)


def extended(cells, sides, width):
    for axis, dim in sides:
        count = lax.axis_size(axis)
        ends = count - 1
        head = lax.slice_in_dim(cells, 0, width, axis=dim)
        tail = lax.slice_in_dim(cells, cells.shape[dim] - width, cells.shape[dim], axis=dim)
        cells = jnp.concatenate(
            [
                lax.ppermute(tail, axis, [(i, (i + 1) % count) for i in range(ends)]),
                cells,
                lax.ppermute(head, axis, [((i + 1) % count, i) for i in range(ends)]),
            ],
            axis=dim,
        )
    return cells


def in_blocks(value, dim, length):
    shape = value.shape
    tiles = value.reshape(*shape[:dim], length, shape[dim] // length, *shape[dim + 1 :])
    return jnp.moveaxis(tiles, dim, 0)


def sum_at_owner(value, axis, dim):
    tiles = in_blocks(value, dim, lax.axis_size(axis))
    arrived = lax.all_to_all(tiles, axis, split_axis=0, concat_axis=0, tiled=True)
    return arrived.astype(jnp.float32).sum(axis=0)


def sent_to_all(value, axis):
    copies = jnp.broadcast_to(value, (lax.axis_size(axis), *value.shape))
    return lax.all_to_all(copies, axis, split_axis=0, concat_axis=0, tiled=True)


def in_order(tiles, dim):
    shape = list(tiles.shape[1:])
    shape[dim] *= tiles.shape[0]
    return jnp.moveaxis(tiles, 0, dim).reshape(shape)


def collect(value, axis, dim):
    tiles = sent_to_all(value, axis)
    return in_order(tiles, dim)


def windows(padded, first, height, width, taps):
    rows = padded[first : first + height]
    return jnp.stack([rows[:, shift : shift + width] for shift in range(taps)], axis=2)


def adam_update(master, moment, second, grad):
    new_moment = 0.9 * moment + 0.1 * grad
    new_second = 0.999 * second + 0.001 * grad * grad
    new_dictionary = master - 0.05 * (new_moment / first_fix) / (
        jnp.sqrt(new_second / second_fix) + 1e-08
    )
    return (new_dictionary, new_moment, new_second)


def adjoint(resid_pad, filters, codes, height, width, taps):
    back = jnp.zeros(codes.shape, jnp.float32)
    for tap_row in range(taps):
        rows = resid_pad[6 - tap_row : 6 - tap_row + height]
        block = jnp.stack([rows[:, 6 - shift : 6 - shift + width] for shift in range(taps)], axis=2)
        back = back + jnp.einsum(
            "ijbc,cbk->ijk", block, filters[:, tap_row], preferred_element_type=jnp.float32
        )
    moved = codes.astype(jnp.float32) - 0.05 * back
    return (moved - jnp.clip(moved, -0.02, 0.02)).astype(jnp.bfloat16)


def correlation(resid, code_pad, height, width, taps):
    tap_terms = []
    for tap_row in range(taps):
        block = windows(code_pad, tap_row, height, width, taps)
        tap_terms.append(
            jnp.einsum("ijc,ijbk->cbk", resid, block, preferred_element_type=jnp.float32)
        )
    return jnp.stack(tap_terms, axis=1)


def local(codes, image, master, moment, second):
    height, width = (codes.shape[0], codes.shape[1])
    taps = master.shape[1]
    filters = gather_axes(master.astype(jnp.bfloat16), ("row", "col"), 0)
    bands = filters.shape[0]
    code_pad = extended(codes, (("row", 0), ("col", 1)), 3)
    share_rows = height // lax.axis_size("atom")
    total = jnp.zeros((share_rows * lax.axis_size("atom"), width, bands), jnp.float32)
    for tap_row in range(taps):
        block = windows(code_pad, tap_row, share_rows * lax.axis_size("atom"), width, taps)
        total = total + jnp.einsum(
            "ijbk,cbk->ijc", block, filters[:, tap_row], preferred_element_type=jnp.float32
        )
    part = sum_at_owner(total.astype(jnp.bfloat16), "atom", 0)
    first_row = lax.axis_index("atom") * share_rows
    own_image = lax.dynamic_slice_in_dim(image, first_row, share_rows, 0)
    piece = (part - own_image.astype(jnp.float32)).astype(jnp.bfloat16)
    resid = collect(piece, "atom", 0)
    resid_pad = extended(resid, (("row", 0), ("col", 1)), 3)
    new_codes = adjoint(resid_pad, filters, codes, height, width, taps)
    tile_term = correlation(resid, code_pad, height, width, taps)
    half = sum_at_owner(tile_term.astype(jnp.bfloat16), "row", 0)
    grad = sum_at_owner(half.astype(jnp.bfloat16), "col", 0)
    new_dictionary, new_moment, new_second = adam_update(master, moment, second, grad)
    return (new_codes, new_dictionary, new_moment, new_second)


def solution(mesh):
    return jax.shard_map(
        local,
        mesh=mesh,
        in_specs=(
            P("row", "col", "atom"),
            P("row", "col", None),
            P(("row", "col"), None, None, "atom"),
            P(("row", "col"), None, None, "atom"),
            P(("row", "col"), None, None, "atom"),
        ),
        out_specs=(
            P("row", "col", "atom"),
            P(("row", "col"), None, None, "atom"),
            P(("row", "col"), None, None, "atom"),
            P(("row", "col"), None, None, "atom"),
        ),
        check_vma=False,
    )
```

profile of v0, /device:TPU:1, one launch (start us, length us, event | category | flops | bytes accessed | tf_op | source)
XLA Modules:
  0.0 204.5 jit_solution(5781954799397815813)
XLA Ops:
  7.2 0.7 fusion.143
  7.9 4.8 %collective-permute-start = (bf16[3,16,128]{2,1,0:T(8,128)(2,1)S(1)}, bf16[3,16,128]{2,1,0:T(8,128)(2,1)S(1)}, u32[]{:S(2)}, u32[]{:S(2)}) collective-permute-start(bf16[3,16,128]{2,1,0:T(8,128)(2,1)S(1)} %get-tuple-element.99), channel_id=1, source_target_pairs={{0,4},{4,8},{8,12},{12,16},{16,20},{20,24},{24,28},{1,5},{5,9},{9,... | collective-permute-start | bytes 36872 | tf_op jit(solution)/shard_map/ppermute | solution.py:25
  12.8 1.3 collective-permute-start.1
  14.1 0.9 convert_element_type.31
  15.0 0.9 constant_dynamic-update-slice_fusion.3
  15.9 1.9 collective-permute-done.1
  17.9 4.2 %collective-permute-start.2 = (bf16[22,3,128]{2,1,0:T(4,128)(2,1)S(1)}, bf16[22,3,128]{2,1,0:T(4,128)(2,1)S(1)}, u32[]{:S(2)}, u32[]{:S(2)}) collective-permute-start(bf16[22,3,128]{2,1,0:T(4,128)(2,1)S(1)} %get-tuple-element.80), channel_id=1, source_target_pairs={{0,1},{1,2},{2,3},{4,5},{5,6},{6,7},{8,9},{9,10},{10,11},{12,13},{... | collective-permute-start | bytes 50696 | tf_op jit(solution)/shard_map/ppermute | solution.py:25
  22.1 12.1 %all_gather.6 = bf16[16,7,7,128]{3,2,1,0:T(8,128)(2,1)S(1)} all-gather(bf16[4,7,7,128]{3,2,1,0:T(8,128)(2,1)S(1)} %copy.87), channel_id=1, replica_groups=mesh['atom'=16,'row'=8,'col'=4] {'col'}, dimensions={0}, use_global_device_ids=true | all-gather | bytes 250880 | tf_op jit(solution)/shard_map/all_gather | solution.py:13
  34.2 0.7 copy.88
  35.0 1.3 collective-permute-start.3
  36.5 4.5 %collective-permute-done.3 = bf16[22,3,128]{2,1,0:T(4,128)(2,1)S(1)} collective-permute-done((bf16[22,3,128]{2,1,0:T(4,128)(2,1)S(1)}, bf16[22,3,128]{2,1,0:T(4,128)(2,1)S(1)}, u32[]{:S(2)}, u32[]{:S(2)}) %collective-permute-start.3) | collective-permute-done | bytes 16928 | tf_op jit(solution)/shard_map/ppermute | solution.py:27
  41.4 0.9 constant_dynamic-update-slice_fusion.15
  43.7 0.8 copy-done.7
  44.5 39.8 %all-gather.2.cloned.1.call-done = bf16[128,7,7,128]{3,0,2,1:T(8,128)(2,1)} async-done(((bf16[16,7,7,128]{3,0,2,1:T(8,128)(2,1)}), bf16[128,7,7,128]{3,0,2,1:T(8,128)(2,1)}) %all-gather.2.cloned.1.call-update) | async-done | bytes 1605648 | tf_op jit(solution)/shard_map/all_gather | solution.py:13
  84.3 1.5 convolution_bitcast_fusion.15
  85.8 1.3 convolution_bitcast_fusion.16
  88.4 0.9 fusion.36
  89.3 10.1 %all-to-all-start = ((bf16[16,1,16,128]{3,2,1,0:T(8,128)(2,1)}), bf16[16,1,16,128]{3,2,1,0:T(8,128)(2,1)S(1)}, u32[]{:S(2)}, u32[]{:S(2)}) async-start(bf16[16,1,16,128]{3,2,1,0:T(8,128)(2,1)} %fusion.36), calls=%async_computation | async-start | bytes 131072 | tf_op jit(solution)/shard_map/all_to_all | solution.py:42
  99.4 5.8 %all-to-all-done = bf16[16,1,16,128]{3,2,1,0:T(8,128)(2,1)S(1)} async-done(((bf16[16,1,16,128]{3,2,1,0:T(8,128)(2,1)}), bf16[16,1,16,128]{3,2,1,0:T(8,128)(2,1)S(1)}, u32[]{:S(2)}, u32[]{:S(2)}) %all-to-all-start) | async-done | bytes 65568 | tf_op jit(solution)/shard_map/all_to_all | solution.py:42
  105.2 0.7 fusion.140
  105.9 8.7 %all_to_all.20 = bf16[16,1,16,128]{3,2,1,0:T(8,128)(2,1)S(1)} all-to-all(bf16[16,1,16,128]{3,2,1,0:T(8,128)(2,1)S(1)} %broadcast_in_dim.3), channel_id=1, replica_groups=mesh['atom'=16,'row'=8,'col'=4] {'atom'}, dimensions={0} | all-to-all | bytes 131072 | tf_op jit(solution)/shard_map/all_to_all | solution.py:48
  115.0 1.2 copy.117
  116.2 1.7 fusion.20
  120.9 2.7 %collective-permute-start.4 = (bf16[3,16,128]{2,1,0:T(8,128)(2,1)S(1)}, bf16[3,16,128]{2,1,0:T(8,128)(2,1)S(1)}, u32[]{:S(2)}, u32[]{:S(2)}) collective-permute-start(bf16[3,16,128]{2,1,0:T(8,128)(2,1)S(1)} %get-tuple-element.93), channel_id=1, source_target_pairs={{0,4},{4,8},{8,12},{12,16},{16,20},{20,24},{24,28},{1,5},{5,9},{9,... | collective-permute-start | bytes 36872 | tf_op jit(solution)/shard_map/ppermute | solution.py:25
  123.6 1.3 collective-permute-start.5
  125.3 2.7 %collective-permute-done.5 = bf16[3,16,128]{2,1,0:T(8,128)(2,1)S(1)} collective-permute-done((bf16[3,16,128]{2,1,0:T(8,128)(2,1)S(1)}, bf16[3,16,128]{2,1,0:T(8,128)(2,1)S(1)}, u32[]{:S(2)}, u32[]{:S(2)}) %collective-permute-start.5) | collective-permute-done | bytes 12320 | tf_op jit(solution)/shard_map/ppermute | solution.py:27
  128.0 1.3 collective-permute-start.6
  129.3 4.9 %collective-permute-start.7 = (bf16[22,3,128]{2,1,0:T(4,128)(2,1)S(1)}, bf16[22,3,128]{2,1,0:T(4,128)(2,1)S(1)}, u32[]{:S(2)}, u32[]{:S(2)}) collective-permute-start(bf16[22,3,128]{2,1,0:T(4,128)(2,1)S(1)} %get-tuple-element.75), channel_id=1, source_target_pairs={{0,1},{1,2},{2,3},{4,5},{5,6},{6,7},{8,9},{9,10},{10,11},{12,13},{... | collective-permute-start | bytes 50696 | tf_op jit(solution)/shard_map/ppermute | solution.py:25
  134.7 1.5 copy.106
  136.1 4.9 %all-to-all-start.2 = ((bf16[8,16,7,7,128]{4,1,3,2,0:T(8,128)(2,1)}), bf16[8,16,7,7,128]{4,1,3,2,0:T(8,128)(2,1)S(1)}, u32[]{:S(2)}, u32[]{:S(2)}) async-start(bf16[8,16,7,7,128]{4,1,3,2,0:T(8,128)(2,1)} %copy.106), calls=%async_computation.2 | async-start | bytes 3211264 | tf_op jit(solution)/shard_map/all_to_all | solution.py:42
  141.1 0.7 constant_dynamic-update-slice_fusion.62
  141.8 0.7 constant_dynamic-update-slice_fusion.61
  142.5 0.7 constant_dynamic-update-slice_fusion.60
  143.3 0.7 constant_dynamic-update-slice_fusion.59
  144.4 0.9 convolution_bitcast_fusion.12
  145.4 0.9 convolution_bitcast_fusion.11
  146.3 0.9 convolution_bitcast_fusion.10
  147.3 0.9 convolution_bitcast_fusion.9
  148.2 0.9 convolution_bitcast_fusion.8
  149.1 0.7 constant_dynamic-update-slice_fusion.58
  149.8 0.7 constant_dynamic-update-slice_fusion.57
  151.1 31.1 %all-to-all-done.2 = bf16[8,16,7,7,128]{4,1,3,2,0:T(8,128)(2,1)S(1)} async-done(((bf16[8,16,7,7,128]{4,1,3,2,0:T(8,128)(2,1)}), bf16[8,16,7,7,128]{4,1,3,2,0:T(8,128)(2,1)S(1)}, u32[]{:S(2)}, u32[]{:S(2)}) %all-to-all-start.2) | async-done | bytes 1605664 | tf_op jit(solution)/shard_map/all_to_all | solution.py:42
  182.4 0.8 copy.108
  183.2 5.7 %all-to-all-start.3 = ((bf16[4,4,7,7,128]{4,1,3,2,0:T(4,128)(2,1)}), bf16[4,4,7,7,128]{4,1,3,2,0:T(4,128)(2,1)S(1)}, u32[]{:S(2)}, u32[]{:S(2)}) async-start(bf16[4,4,7,7,128]{4,1,3,2,0:T(4,128)(2,1)} %copy.108), calls=%async_computation.3 | async-start | bytes 401408 | tf_op jit(solution)/shard_map/all_to_all | solution.py:42
  188.9 1.3 convolution_bitcast_fusion.7
  190.2 2.0 fusion.45
  192.2 4.5 %all-to-all-done.3 = bf16[4,4,7,7,128]{4,1,3,2,0:T(4,128)(2,1)S(1)} async-done(((bf16[4,4,7,7,128]{4,1,3,2,0:T(4,128)(2,1)}), bf16[4,4,7,7,128]{4,1,3,2,0:T(4,128)(2,1)S(1)}, u32[]{:S(2)}, u32[]{:S(2)}) %all-to-all-start.3) | async-done | bytes 200736 | tf_op jit(solution)/shard_map/all_to_all | solution.py:42
  196.8 0.8 divide_subtract_fusion
  (107 shorter events, 9.1 us)
Async XLA Ops:
  7.2 77.1 %all-gather.2.cloned.1.call-start = ((), (), s32[]{:S(2)}) async-start(), calls=%async_computation.4 | async-start | bytes 1806336 | tf_op jit(solution)/shard_map/all_gather | solution.py:13
  7.9 7.1 %collective-permute-start = (bf16[3,16,128]{2,1,0:T(8,128)(2,1)S(1)}, bf16[3,16,128]{2,1,0:T(8,128)(2,1)S(1)}, u32[]{:S(2)}, u32[]{:S(2)}) collective-permute-start(bf16[3,16,128]{2,1,0:T(8,128)(2,1)S(1)} %get-tuple-element.99), channel_id=1, source_target_pairs={{0,4},{4,8},{8,12},{12,16},{16,20},{20,24},{24,28},{1,5},{5,9},{9,... | collective-permute-start | bytes 36872 | tf_op jit(solution)/shard_map/ppermute | solution.py:25
  12.8 5.1 %collective-permute-start.1 = (bf16[3,16,128]{2,1,0:T(8,128)(2,1)S(1)}, bf16[3,16,128]{2,1,0:T(8,128)(2,1)S(1)}, u32[]{:S(2)}, u32[]{:S(2)}) collective-permute-start(bf16[3,16,128]{2,1,0:T(8,128)(2,1)S(1)} %get-tuple-element.98), channel_id=1, source_target_pairs={{4,0},{8,4},{12,8},{16,12},{20,16},{24,20},{28,24},{5,1},{9,5},{13... | collective-permute-start | bytes 36872 | tf_op jit(solution)/shard_map/ppermute | solution.py:27
  15.9 2.0 copy-start.14
  17.9 18.4 %collective-permute-start.2 = (bf16[22,3,128]{2,1,0:T(4,128)(2,1)S(1)}, bf16[22,3,128]{2,1,0:T(4,128)(2,1)S(1)}, u32[]{:S(2)}, u32[]{:S(2)}) collective-permute-start(bf16[22,3,128]{2,1,0:T(4,128)(2,1)S(1)} %get-tuple-element.80), channel_id=1, source_target_pairs={{0,1},{1,2},{2,3},{4,5},{5,6},{6,7},{8,9},{9,10},{10,11},{12,13},{... | collective-permute-start | bytes 50696 | tf_op jit(solution)/shard_map/ppermute | solution.py:25
  34.2 7.2 %copy-start.1 = (bf16[16,16,128]{2,1,0:T(8,128)(2,1)S(1)}, bf16[16,16,128]{2,1,0:T(8,128)(2,1)}, u32[]{:S(2)}) copy-start(bf16[16,16,128]{2,1,0:T(8,128)(2,1)} %param.5) | copy-start | bytes 196612
  35.0 6.1 %collective-permute-start.3 = (bf16[22,3,128]{2,1,0:T(4,128)(2,1)S(1)}, bf16[22,3,128]{2,1,0:T(4,128)(2,1)S(1)}, u32[]{:S(2)}, u32[]{:S(2)}) collective-permute-start(bf16[22,3,128]{2,1,0:T(4,128)(2,1)S(1)} %get-tuple-element.79), channel_id=1, source_target_pairs={{1,0},{2,1},{3,2},{5,4},{6,5},{7,6},{9,8},{10,9},{11,10},{13,12},{... | collective-permute-start | bytes 50696 | tf_op jit(solution)/shard_map/ppermute | solution.py:27
  36.5 6.1 %copy-start.15 = (bf16[19,16,128]{2,1,0:T(8,128)(2,1)S(1)}, bf16[19,16,128]{2,1,0:T(8,128)(2,1)}, u32[]{:S(2)}) copy-start(bf16[19,16,128]{2,1,0:T(8,128)(2,1)} %copy-done.14) | copy-start | bytes 233476
  42.8 0.8 copy-start.12
  42.9 0.8 copy-start.9
  43.7 0.8 copy-start.7
  44.5 43.2 %copy-start.3 = (bf16[16,16,7,128]{3,1,0,2:T(8,128)(2,1)}, bf16[16,16,7,128]{3,1,0,2:T(8,128)(2,1)S(1)}, u32[]{:S(2)}) copy-start(bf16[16,16,7,128]{3,1,0,2:T(8,128)(2,1)S(1)} %get-tuple-element.66) | copy-start | bytes 1376260
  44.5 61.4 %copy-start.5 = (bf16[16,16,7,128]{3,1,0,2:T(8,128)(2,1)}, bf16[16,16,7,128]{3,1,0,2:T(8,128)(2,1)S(1)}, u32[]{:S(2)}) copy-start(bf16[16,16,7,128]{3,1,0,2:T(8,128)(2,1)S(1)} %get-tuple-element.67) | copy-start | bytes 1376260
  84.3 2.8 %copy-start = (bf16[128,7,7,128]{3,0,2,1:T(8,128)(2,1)S(1)}, bf16[128,7,7,128]{3,0,2,1:T(8,128)(2,1)}, u32[]{:S(2)}) copy-start(bf16[128,7,7,128]{3,0,2,1:T(8,128)(2,1)} %all-gather.2.cloned.1.call-done) | copy-start | bytes 4816900
  84.3 3.5 %copy-start.10 = (bf16[16,16,7,128]{3,1,0,2:T(8,128)(2,1)S(1)}, bf16[16,16,7,128]{3,1,0,2:T(8,128)(2,1)}, u32[]{:S(2)}) copy-start(bf16[16,16,7,128]{3,1,0,2:T(8,128)(2,1)} %copy-done.9) | copy-start | bytes 1376260
  85.8 2.2 %copy-start.13 = (bf16[16,16,7,128]{3,1,2,0:T(8,128)(2,1)S(1)}, bf16[16,16,7,128]{3,1,2,0:T(8,128)(2,1)}, u32[]{:S(2)}) copy-start(bf16[16,16,7,128]{3,1,2,0:T(8,128)(2,1)} %copy-done.12) | copy-start | bytes 1376260
  89.3 15.9 %all-to-all-start = ((bf16[16,1,16,128]{3,2,1,0:T(8,128)(2,1)}), bf16[16,1,16,128]{3,2,1,0:T(8,128)(2,1)S(1)}, u32[]{:S(2)}, u32[]{:S(2)}) async-start(bf16[16,1,16,128]{3,2,1,0:T(8,128)(2,1)} %fusion.36), calls=%async_computation | async-start | bytes 131072 | tf_op jit(solution)/shard_map/all_to_all | solution.py:42
  116.2 1.7 copy-start.11
  116.2 1.7 copy-start.21
  118.4 1.0 copy-start.4
  119.4 1.0 copy-start.6
  120.4 4.5 %copy-start.8 = (bf16[16,16,7,128]{3,1,0,2:T(8,128)(2,1)S(1)}, bf16[16,16,7,128]{3,1,0,2:T(8,128)(2,1)}, u32[]{:S(2)}) copy-start(bf16[16,16,7,128]{3,1,0,2:T(8,128)(2,1)} %copy-done.7) | copy-start | bytes 1376260
  120.9 4.5 %collective-permute-start.4 = (bf16[3,16,128]{2,1,0:T(8,128)(2,1)S(1)}, bf16[3,16,128]{2,1,0:T(8,128)(2,1)S(1)}, u32[]{:S(2)}, u32[]{:S(2)}) collective-permute-start(bf16[3,16,128]{2,1,0:T(8,128)(2,1)S(1)} %get-tuple-element.93), channel_id=1, source_target_pairs={{0,4},{4,8},{8,12},{12,16},{16,20},{20,24},{24,28},{1,5},{5,9},{9,... | collective-permute-start | bytes 36872 | tf_op jit(solution)/shard_map/ppermute | solution.py:25
  123.6 4.4 %collective-permute-start.5 = (bf16[3,16,128]{2,1,0:T(8,128)(2,1)S(1)}, bf16[3,16,128]{2,1,0:T(8,128)(2,1)S(1)}, u32[]{:S(2)}, u32[]{:S(2)}) collective-permute-start(bf16[3,16,128]{2,1,0:T(8,128)(2,1)S(1)} %get-tuple-element.94), channel_id=1, source_target_pairs={{4,0},{8,4},{12,8},{16,12},{20,16},{24,20},{28,24},{5,1},{9,5},{13... | collective-permute-start | bytes 36872 | tf_op jit(solution)/shard_map/ppermute | solution.py:27
  128.0 13.0 %collective-permute-start.6 = (bf16[22,3,128]{2,1,0:T(4,128)(2,1)S(1)}, bf16[22,3,128]{2,1,0:T(4,128)(2,1)S(1)}, u32[]{:S(2)}, u32[]{:S(2)}) collective-permute-start(bf16[22,3,128]{2,1,0:T(4,128)(2,1)S(1)} %get-tuple-element.76), channel_id=1, source_target_pairs={{1,0},{2,1},{3,2},{5,4},{6,5},{7,6},{9,8},{10,9},{11,10},{13,12},{... | collective-permute-start | bytes 50696 | tf_op jit(solution)/shard_map/ppermute | solution.py:27
  129.3 11.7 %collective-permute-start.7 = (bf16[22,3,128]{2,1,0:T(4,128)(2,1)S(1)}, bf16[22,3,128]{2,1,0:T(4,128)(2,1)S(1)}, u32[]{:S(2)}, u32[]{:S(2)}) collective-permute-start(bf16[22,3,128]{2,1,0:T(4,128)(2,1)S(1)} %get-tuple-element.75), channel_id=1, source_target_pairs={{0,1},{1,2},{2,3},{4,5},{5,6},{6,7},{8,9},{9,10},{10,11},{12,13},{... | collective-permute-start | bytes 50696 | tf_op jit(solution)/shard_map/ppermute | solution.py:25
  136.1 46.0 %all-to-all-start.2 = ((bf16[8,16,7,7,128]{4,1,3,2,0:T(8,128)(2,1)}), bf16[8,16,7,7,128]{4,1,3,2,0:T(8,128)(2,1)S(1)}, u32[]{:S(2)}, u32[]{:S(2)}) async-start(bf16[8,16,7,7,128]{4,1,3,2,0:T(8,128)(2,1)} %copy.106), calls=%async_computation.2 | async-start | bytes 3211264 | tf_op jit(solution)/shard_map/all_to_all | solution.py:42
  144.4 3.7 %copy-start.2 = (bf16[16,16,7,128]{3,1,0,2:T(8,128)(2,1)}, bf16[16,16,7,128]{3,1,0,2:T(8,128)(2,1)S(1)}, u32[]{:S(2)}) copy-start(bf16[16,16,7,128]{3,1,0,2:T(8,128)(2,1)S(1)} %get-tuple-element.8) | copy-start | bytes 1376260
  182.4 7.8 %copy-start.16 = (f32[16,16,128]{2,1,0:T(8,128)S(1)}, f32[16,16,128]{2,1,0:T(8,128)}, u32[]{:S(2)}) copy-start(f32[16,16,128]{2,1,0:T(8,128)} %convolution_bitcast_fusion.12) | copy-start | bytes 393220
  182.4 7.8 %copy-start.17 = (f32[16,16,128]{2,1,0:T(8,128)S(1)}, f32[16,16,128]{2,1,0:T(8,128)}, u32[]{:S(2)}) copy-start(f32[16,16,128]{2,1,0:T(8,128)} %convolution_bitcast_fusion.11) | copy-start | bytes 393220
  182.4 7.8 %copy-start.18 = (f32[16,16,128]{2,1,0:T(8,128)S(1)}, f32[16,16,128]{2,1,0:T(8,128)}, u32[]{:S(2)}) copy-start(f32[16,16,128]{2,1,0:T(8,128)} %convolution_bitcast_fusion.10) | copy-start | bytes 393220
  182.4 7.8 %copy-start.19 = (f32[16,16,128]{2,1,0:T(8,128)S(1)}, f32[16,16,128]{2,1,0:T(8,128)}, u32[]{:S(2)}) copy-start(f32[16,16,128]{2,1,0:T(8,128)} %convolution_bitcast_fusion.9) | copy-start | bytes 393220
  182.4 7.8 %copy-start.20 = (f32[16,16,128]{2,1,0:T(8,128)S(1)}, f32[16,16,128]{2,1,0:T(8,128)}, u32[]{:S(2)}) copy-start(f32[16,16,128]{2,1,0:T(8,128)} %convolution_bitcast_fusion.8) | copy-start | bytes 393220
  183.2 13.6 %copy-start.22 = (f32[4,7,7,128]{3,0,2,1:T(4,128)S(1)}, f32[4,7,7,128]{3,0,2,1:T(4,128)}, u32[]{:S(2)}) copy-start(f32[4,7,7,128]{3,0,2,1:T(4,128)} %param.7) | copy-start | bytes 301060
  183.2 13.6 %copy-start.23 = (f32[4,7,7,128]{3,0,2,1:T(4,128)S(1)}, f32[4,7,7,128]{3,0,2,1:T(4,128)}, u32[]{:S(2)}) copy-start(f32[4,7,7,128]{3,0,2,1:T(4,128)} %param.8) | copy-start | bytes 301060
  183.2 13.6 %copy-start.24 = (f32[4,7,7,128]{3,0,2,1:T(4,128)S(1)}, f32[4,7,7,128]{3,0,2,1:T(4,128)}, u32[]{:S(2)}) copy-start(f32[4,7,7,128]{3,0,2,1:T(4,128)} %param.9) | copy-start | bytes 301060
  183.2 13.5 %all-to-all-start.3 = ((bf16[4,4,7,7,128]{4,1,3,2,0:T(4,128)(2,1)}), bf16[4,4,7,7,128]{4,1,3,2,0:T(4,128)(2,1)S(1)}, u32[]{:S(2)}, u32[]{:S(2)}) async-start(bf16[4,4,7,7,128]{4,1,3,2,0:T(4,128)(2,1)} %copy.108), calls=%async_computation.3 | async-start | bytes 401408 | tf_op jit(solution)/shard_map/all_to_all | solution.py:42
Sparse Core Ops, SparseCore 0:
  35.1 49.1 all-gather.1
where the time goes:
time: 206 us; the launch traced here: 204 us
  waiting for transfers between devices  90.3 us (44%)
  starting transfers between devices  42.4 us (21%)
  blocking collectives  20.8 us (10%)
  matrix products  17.1 us (8%)
  between operations  14.6 us (7%)
  local copies, waits for them, and re-layouts  14.4 us (7%)
  other arithmetic  4.67 us (2%)
    all_to_all x3, waiting for transfers between devices, sum_at_owner(): lax.all_to_all(tiles, axis, split_axis=0, concat_axis=0, tiled=True)  41.4 us
    all_gather x1, waiting for transfers between devices, gather_axes(): nearer = lax.all_gather(value, axes[-1], axis=dim, tiled=True)  39.8 us
    all_to_all x3, starting transfers between devices, sum_at_owner(): lax.all_to_all(tiles, axis, split_axis=0, concat_axis=0, tiled=True)  20.6 us
    ppermute x4, starting transfers between devices, extended(): lax.ppermute(tail, axis, [(i, (i + 1) % count) for i in range(ends)])  16.6 us
    all_gather x1, blocking collectives, gather_axes(): nearer = lax.all_gather(value, axes[-1], axis=dim, tiled=True)  12.1 us
    ppermute x4, waiting for transfers between devices, extended(): lax.ppermute(head, axis, [((i + 1) % count, i) for i in range(ends)])  9.11 us
    all_to_all x1, blocking collectives, sent_to_all(): return lax.all_to_all(copies, axis, split_axis=0, concat_axis=0, tiled=True)  8.72 us
    dot_general x7, matrix products, adjoint(): jnp.einsum('ijbc,cbk->ijk', block, filters[:, tap_row], preferred_element...  7.89 us
  transfers between devices with their start and end apart: 12, of which 7 were waited for; matrix products, arithmetic and copies ran while one was open for 10% of the time, Pallas kernels for 0%

commit v1 on v0

v1 whole, which is shorter than its diff:
```python
import jax
import jax.numpy as jnp
from jax import lax
from jax.experimental import pallas as pl
from jax.experimental.pallas import tpu as pltpu
from jax.sharding import PartitionSpec as P

MESH = pl.DeviceIdType.MESH
F32, BF16 = jnp.float32, jnp.bfloat16
first_fix = 0.9999734386011124
second_fix = 0.09520785288629038
ROWS, COLS, ATOMS = 8, 4, 16
TAPS = 7


def kernel(
    codes, image, master, moment, second,
    out_codes, out_dict, out_moment, out_second,
    x_buf, x7, f_buf, f_scr, m_buf, mo_buf, se_buf,
    img_in, img_out, img_got,
    pt, halo_out, halo_got, part_out, part_got,
    resid, edge_got, xr, xrb,
    g_out, g_got, p2, bk_out, bk_got, g_scr,
    in_sem, f_send, f_recv, c_send, c_recv, i_send, i_recv,
    h_send, h_recv, p_send, p_recv, r_send, r_recv, e_send, e_recv,
    g_send, g_recv, b_send, b_recv,
):
    r = lax.axis_index("row")
    q = lax.axis_index("col")
    t = lax.axis_index("atom")
    pair, half = t // 2, lax.rem(t, 2)

    def remote(src, dst, send, recv, who):
        return pltpu.make_async_remote_copy(
            src_ref=src, dst_ref=dst, send_sem=send, recv_sem=recv,
            device_id=who, device_id_type=MESH,
        )

    in_m = pltpu.make_async_copy(master, m_buf, in_sem.at[0])
    in_c = pltpu.make_async_copy(codes, x_buf.at[:, pl.ds(pl.multiple_of(q * 16, 16), 16)], in_sem.at[1])
    in_i = pltpu.make_async_copy(image.at[pl.ds(2 * pair, 2)], img_in, in_sem.at[2])
    in_mo = pltpu.make_async_copy(moment, mo_buf, in_sem.at[3])
    in_se = pltpu.make_async_copy(second, se_buf, in_sem.at[4])
    for copy in (in_m, in_c, in_i, in_mo, in_se):
        copy.start()

    barrier = pltpu.get_barrier_semaphore()
    for axis, size, me in (("row", ROWS, r), ("col", COLS, q), ("atom", ATOMS, t)):
        for d in range(1, size):
            pl.semaphore_signal(barrier, inc=1, device_id={axis: lax.rem(me + d, size)}, device_id_type=MESH)

    f_scr[...] = jnp.zeros_like(f_scr)
    in_m.wait()
    for i in range(4):
        for a in range(TAPS):
            f_scr[pl.ds((i * 8 + a) * 8, TAPS), :] = m_buf[i, a]
    for b in range(TAPS):
        f_buf[r, :, b * 128 : (b + 1) * 128] = f_scr[pl.ds(b, 32, stride=8), :].astype(BF16)

    pl.semaphore_wait(barrier, ROWS + COLS + ATOMS - 3)

    f_copies = []
    for d in range(1, ROWS):
        f_copies.append(
            remote(f_buf.at[r], f_buf.at[r], f_send.at[d - 1], f_recv.at[d - 1], {"row": lax.rem(r + d, ROWS)})
        )
        f_copies[-1].start()
    in_c.wait()
    own = x_buf.at[:, pl.ds(pl.multiple_of(q * 16, 16), 16)]
    c_copies = []
    for d in range(1, COLS):
        c_copies.append(remote(own, own, c_send.at[d - 1], c_recv.at[d - 1], {"col": lax.rem(q + d, COLS)}))
        c_copies[-1].start()

    in_i.wait()
    n = lax.broadcasted_iota(jnp.int32, (64, 128), 0)
    lane = lax.broadcasted_iota(jnp.int32, (64, 128), 1)
    band = (4 * half + ((n >> 2) & 3)) * 16 + (n >> 4) * 4 + (n & 3)
    pick = jnp.where(lane == band, 1.0, 0.0).astype(BF16)
    picked = lax.dot_general(
        pick, img_in[...].reshape(32, 128), (((1,), (1,)), ((), ())), preferred_element_type=F32
    ).astype(BF16)
    n = lax.broadcasted_iota(jnp.int32, (32, 128), 0)
    lane = lax.broadcasted_iota(jnp.int32, (32, 128), 1)
    place = jnp.where(lane == (n >> 4) * 64 + q * 16 + (n & 15), 1.0, 0.0).astype(BF16)
    img_out[...] = jnp.dot(picked, place, preferred_element_type=F32).astype(BF16).reshape(COLS, 16, 128)
    i_copies = []
    for d in range(1, COLS):
        to = lax.rem(q + d, COLS)
        i_copies.append(remote(img_out.at[to], img_got.at[d - 1], i_send.at[d - 1], i_recv.at[d - 1], {"col": to}))
        i_copies[-1].start()

    for copy in c_copies:
        copy.wait_recv()

    v = lax.broadcasted_iota(jnp.int32, (64, 128), 0)

    def shift_codes(u, carry):
        x = x_buf[u].astype(F32)
        for b in range(TAPS):
            s = b - 3
            moved = x if s == 0 else pltpu.roll(x, (-s) % 64, 0)
            if s:
                moved = jnp.where((v + s >= 0) & (v + s < 64), moved, 0.0)
            x7[pl.ds(pl.multiple_of(u * 64, 64), 64), b * 128 : (b + 1) * 128] = moved.astype(BF16)
        return carry

    lax.fori_loop(0, 16, shift_codes, 0)
    for copy in f_copies:
        copy.wait_recv()

    filters = f_buf[...].reshape(256, 896)
    product = lax.dot_general(filters, x7[...], (((1,), (1,)), ((), ())), preferred_element_type=F32)
    for j in range(8):
        pt[j] = product[:, j * 128 : (j + 1) * 128]

    lane = lax.broadcasted_iota(jnp.int32, (32, 128), 1)

    def swapped(x):
        return pltpu.roll(x, 64, 1)

    def tap(a, j):
        return pt[j, pl.ds(a, 32, stride=8), :]

    def add_taps(j, first):
        total = None
        for a in range(first, TAPS, 2):
            at = j - (6 + first - a) // 2
            if 0 <= at < 8:
                total = tap(a, at) if total is None else total + tap(a, at)
        return total if total is not None else jnp.zeros((32, 128), F32)

    evens = {}

    def even(j):
        if j not in evens:
            evens[j] = swapped(add_taps(j, 0)) if 0 <= j < 12 else jnp.zeros((32, 128), F32)
        return evens[j]

    def synth_tile(j):
        return add_taps(j, 1) + jnp.where(lane < 64, even(j - 1), even(j))

    above, below = lax.rem(r + ROWS - 1, ROWS), lax.rem(r + 1, ROWS)
    for at, j in enumerate((0, 1)):
        halo_out[0, at] = synth_tile(j).astype(BF16)
    to_above = remote(halo_out.at[0], halo_got.at[0], h_send.at[0], h_recv.at[0], {"row": above})
    to_above.start()
    for at, j in enumerate((10, 11)):
        halo_out[1, at] = synth_tile(j).astype(BF16)
    to_below = remote(halo_out.at[1], halo_got.at[1], h_send.at[1], h_recv.at[1], {"row": below})
    to_below.start()
    not_first = jnp.where(r > 0, 1.0, 0.0).astype(F32)
    not_last = jnp.where(r < ROWS - 1, 1.0, 0.0).astype(F32)
    mains = [synth_tile(2 + p) for p in range(8)]

    def put(p, value):
        part_out[2 * p] = value[:16].astype(BF16)
        part_out[2 * p + 1] = value[16:].astype(BF16)

    for p in range(2, 6):
        put(p, mains[p])
    to_above.wait_recv()
    for at in range(2):
        put(6 + at, mains[6 + at] + not_last * halo_got[0, at].astype(F32))
    to_below.wait_recv()
    for at in range(2):
        put(at, mains[at] + not_first * halo_got[1, at].astype(F32))
    p_copies = []
    for d in range(1, ATOMS):
        to = lax.rem(t + d, ATOMS)
        p_copies.append(remote(part_out.at[to], part_got.at[d - 1], p_send.at[d - 1], p_recv.at[d - 1], {"atom": to}))
        p_copies[-1].start()
    for copy in i_copies:
        copy.wait_recv()
    own_image = img_out[q].astype(F32)
    for d in range(COLS - 1):
        own_image = own_image + img_got[d].astype(F32)
    for copy in p_copies:
        copy.wait_recv()
    synth = part_out[t].astype(F32)
    for d in range(ATOMS - 1):
        synth = synth + part_got[d].astype(F32)
    resid[t] = (synth - own_image).astype(BF16)
    r_copies = []
    for d in range(1, ATOMS):
        to = lax.rem(t + d, ATOMS)
        r_copies.append(remote(resid.at[t], resid.at[t], r_send.at[d - 1], r_recv.at[d - 1], {"atom": to}))
        r_copies[-1].start()
    for copy in r_copies:
        copy.wait_recv()
    e_copies = [
        remote(resid.at[pl.ds(0, 4)], edge_got.at[1], e_send.at[0], e_recv.at[0], {"row": above}),
        remote(resid.at[pl.ds(12, 4)], edge_got.at[0], e_send.at[1], e_recv.at[1], {"row": below}),
    ]
    for copy in e_copies:
        copy.start()

    def tile_of(ref, p):
        return jnp.concatenate([ref[2 * p], ref[2 * p + 1]], axis=0).astype(F32)

    tiles = {2 + p: tile_of(resid, p) for p in range(8)}
    for copy in e_copies:
        copy.wait_recv()
    for at in range(2):
        tiles[at] = not_first * tile_of(edge_got.at[0], at)
        tiles[10 + at] = not_last * tile_of(edge_got.at[1], at)
    turned = {j: swapped(tiles[j]) for j in range(12)}
    between = {j: jnp.where(lane < 64, turned[j], turned[j + 1]) for j in range(11)}
    for a in range(8):
        for j in range(8):
            tile = tiles[j + (7 - a) // 2] if a % 2 else between[j + (6 - a) // 2]
            xr[j, pl.ds(a, 32, stride=8), :] = tile
    for j in range(8):
        xrb[:, j * 128 : (j + 1) * 128] = xr[j].astype(BF16)

    grad = jnp.dot(xrb[...], x7[...], preferred_element_type=F32)
    g_out[...] = grad.astype(BF16).reshape(ROWS, 32, 896)
    g_copies = []
    for d in range(1, ROWS):
        to = lax.rem(r + d, ROWS)
        g_copies.append(remote(g_out.at[to], g_got.at[d - 1], g_send.at[d - 1], g_recv.at[d - 1], {"row": to}))
        g_copies[-1].start()

    p2[...] = lax.dot_general(
        xrb[...], f_buf[...].reshape(256, 896), (((0,), (0,)), ((), ())), preferred_element_type=F32
    )

    def shift_back(u, carry):
        total = p2[pl.ds(pl.multiple_of(u * 64, 64), 64), 384:512]
        for b in range(TAPS):
            s = b - 3
            if s:
                x = p2[pl.ds(pl.multiple_of(u * 64, 64), 64), b * 128 : (b + 1) * 128]
                moved = pltpu.roll(x, s % 64, 0)
                total = total + jnp.where((v - s >= 0) & (v - s < 64), moved, 0.0)
        bk_out[u] = total.astype(BF16)
        return carry

    lax.fori_loop(0, 16, shift_back, 0)
    b_copies = []
    for d in range(1, COLS):
        to = lax.rem(q + d, COLS)
        b_copies.append(
            remote(
                bk_out.at[:, pl.ds(pl.multiple_of(to * 16, 16), 16)],
                bk_got.at[d - 1], b_send.at[d - 1], b_recv.at[d - 1], {"col": to},
            )
        )
        b_copies[-1].start()
    for copy in b_copies:
        copy.wait_recv()
    mine = pl.ds(pl.multiple_of(q * 16, 16), 16)

    def shrink(u, carry):
        back = bk_out[u, mine].astype(F32)
        for d in range(COLS - 1):
            back = back + bk_got[d, u].astype(F32)
        moved = x_buf[u, mine].astype(F32) - 0.05 * back
        out_codes[u] = (moved - jnp.clip(moved, -0.02, 0.02)).astype(BF16)
        return carry

    lax.fori_loop(0, 16, shrink, 0)

    in_mo.wait()
    in_se.wait()
    for copy in g_copies:
        copy.wait_recv()
    for b in range(TAPS):
        cols = slice(b * 128, (b + 1) * 128)
        total = g_out[r, :, cols].astype(F32)
        for d in range(ROWS - 1):
            total = total + g_got[d, :, cols].astype(F32)
        g_scr[pl.ds(b, 32, stride=8), :] = total
    for i in range(4):
        for a in range(TAPS):
            grad = g_scr[pl.ds((i * 8 + a) * 8, TAPS), :]
            new_moment = 0.9 * mo_buf[i, a] + 0.1 * grad
            new_second = 0.999 * se_buf[i, a] + 0.001 * grad * grad
            out_moment[i, a] = new_moment
            out_second[i, a] = new_second
            out_dict[i, a] = m_buf[i, a] - 0.05 * (new_moment / first_fix) / (
                jnp.sqrt(new_second / second_fix) + 1e-08
            )

    for copy in f_copies + c_copies + i_copies + [to_above, to_below] + p_copies + r_copies + e_copies + g_copies + b_copies:
        copy.wait_send()


def local(codes, image, master, moment, second):
    dma = pltpu.SemaphoreType.DMA
    vmem = pltpu.VMEM
    any_spec = pl.BlockSpec(memory_space=pl.ANY)
    vmem_spec = pl.BlockSpec(memory_space=vmem)
    return pl.pallas_call(
        kernel,
        out_shape=(
            jax.ShapeDtypeStruct(codes.shape, BF16),
            jax.ShapeDtypeStruct(master.shape, F32),
            jax.ShapeDtypeStruct(master.shape, F32),
            jax.ShapeDtypeStruct(master.shape, F32),
        ),
        in_specs=[any_spec] * 5,
        out_specs=(vmem_spec,) * 4,
        scratch_shapes=[
            vmem((16, 64, 128), BF16),
            vmem((1024, 896), BF16),
            vmem((8, 32, 896), BF16),
            vmem((256, 128), F32),
            vmem(master.shape, F32),
            vmem(master.shape, F32),
            vmem(master.shape, F32),
            vmem((2, 16, 128), BF16),
            vmem((4, 16, 128), BF16),
            vmem((3, 16, 128), BF16),
            vmem((8, 256, 128), F32),
            vmem((2, 2, 32, 128), BF16),
            vmem((2, 2, 32, 128), BF16),
            vmem((16, 16, 128), BF16),
            vmem((15, 16, 128), BF16),
            vmem((16, 16, 128), BF16),
            vmem((2, 4, 16, 128), BF16),
            vmem((8, 256, 128), F32),
            vmem((256, 1024), BF16),
            vmem((8, 32, 896), BF16),
            vmem((7, 32, 896), BF16),
            vmem((1024, 896), F32),
            vmem((16, 64, 128), BF16),
            vmem((3, 16, 16, 128), BF16),
            vmem((256, 128), F32),
            dma((5,)),
            dma((7,)), dma((7,)), dma((3,)), dma((3,)), dma((3,)), dma((3,)),
            dma((2,)), dma((2,)), dma((15,)), dma((15,)), dma((15,)), dma((15,)), dma((2,)), dma((2,)),
            dma((7,)), dma((7,)), dma((3,)), dma((3,)),
        ],
        compiler_params=pltpu.CompilerParams(
            collective_id=0, has_side_effects=True, vmem_limit_bytes=40 * 1024 * 1024
        ),
        name="dictionary_step",
    )(codes, image, master, moment, second)


def solution(mesh):
    tile = P("row", "col", "atom")
    bank = P(("row", "col"), None, None, "atom")
    return jax.shard_map(
        local,
        mesh=mesh,
        in_specs=(tile, P("row", "col", None), bank, bank, bank),
        out_specs=(tile, bank, bank, bank),
        check_vma=False,
    )
```

time: 206 us -> 64.4 us (0.31)
  waiting for transfers between devices: 90.3 us -> 0 us
  Pallas kernels: 0 us -> 58.1 us
  starting transfers between devices: 42.4 us -> 0 us
  blocking collectives: 20.8 us -> 0 us
  matrix products: 17.1 us -> 0 us
  between operations: 14.6 us -> 0.68 us
  local copies, waits for them, and re-layouts: 14.4 us -> 5.33 us
  other arithmetic: 4.67 us -> 0 us
    pallas_call x0 -> x1, Pallas kernels: none -> 58.1 us  [local(): pl.pallas_call(kernel, out_shape=(jax.ShapeDtypeStruct(codes.shape, BF16)...]
    all_to_all x3 -> x0, waiting for transfers between devices: 41.4 us -> none  [sum_at_owner(): lax.all_to_all(tiles, axis, split_axis=0, concat_axis=0, tiled=True)]
    all_gather x1 -> x0, waiting for transfers between devices: 39.8 us -> none  [gather_axes(): nearer = lax.all_gather(value, axes[-1], axis=dim, tiled=True)]
    ppermute x8 -> x0, starting transfers between devices: 21.8 us -> none  [the longest x4 16.6 us: extended(): lax.ppermute(tail, axis, [(i, (i + 1) % count) for i in range(ends)])]
    all_to_all x3 -> x0, starting transfers between devices: 20.6 us -> none  [sum_at_owner(): lax.all_to_all(tiles, axis, split_axis=0, concat_axis=0, tiled=True)]
    dot_general x21 -> x0, matrix products: 17.1 us -> none  [the longest x7 7.89 us: adjoint(): jnp.einsum('ijbc,cbk->ijk', block, filters[:, tap_row], preferred_element...]
    all_gather x1 -> x0, blocking collectives: 12.1 us -> none  [gather_axes(): nearer = lax.all_gather(value, axes[-1], axis=dim, tiled=True)]
    ppermute x8 -> x0, waiting for transfers between devices: 9.12 us -> none  [the longest x4 9.11 us: extended(): lax.ppermute(head, axis, [((i + 1) % count, i) for i in range(ends)])]
  transfers between devices with their start and end apart: 12 -> 0, of which waited for: 7 -> 0; matrix products, arithmetic and copies ran while one was open for 10% -> 0% of each run, Pallas kernels for 0% -> 0%
where the time goes in v1:
time: 64.4 us; the launch traced here: 64.1 us
  Pallas kernels  58.1 us (90%)
  local copies, waits for them, and re-layouts  5.33 us (8%)
  between operations  0.68 us (1%)
    pallas_call x1, Pallas kernels, local(): pl.pallas_call(kernel, out_shape=(jax.ShapeDtypeStruct(codes.shape, BF16)...  58.1 us
    unnamed x12, local copies, waits for them, and re-layouts  3.33 us
    pallas_call x3, local copies, waits for them, and re-layouts, local(): pl.pallas_call(kernel, out_shape=(jax.ShapeDtypeStruct(codes.shape, BF16)...  2 us

profile of v1, /device:TPU:1, one launch (start us, length us, event | category | flops | bytes accessed | tf_op | source)
XLA Modules:
  0.0 64.1 jit_solution(15817944626328722105)
XLA Ops:
  0.6 0.0 copy-start.2
  0.6 0.9 %copy.9.master = f32[4,7,7,128]{3,2,1,0:T(8,128)S(1)} copy(f32[4,7,7,128]{3,0,2,1:T(4,128)} %param.7) | data formatting | bytes 200704 | tf_op args[2]
  1.6 0.0 copy-done.2
  1.6 0.0 copy-start.3
  1.6 0.9 %copy-done.3 = f32[4,7,7,128]{3,0,2,1:T(4,128)S(1)} copy-done((f32[4,7,7,128]{3,0,2,1:T(4,128)S(1)}, f32[4,7,7,128]{3,0,2,1:T(4,128)}, u32[]{:S(2)}) %copy-start.3) | copy-done | bytes 100376
  2.5 0.0 copy-start
  2.5 0.0 copy-start.1
  2.5 0.8 %copy-done = bf16[16,16,128]{2,1,0:T(8,128)(2,1)S(1)} copy-done((bf16[16,16,128]{2,1,0:T(8,128)(2,1)S(1)}, bf16[16,16,128]{2,1,0:T(8,128)(2,1)}, u32[]{:S(2)}) %copy-start) | copy-done | bytes 65560
  3.3 0.0 copy-done.1
  3.4 58.1 %dictionary_step.1 = (bf16[16,16,128]{2,1,0:T(8,128)(2,1)S(1)}, f32[4,7,7,128]{3,2,1,0:T(8,128)S(1)}, f32[4,7,7,128]{3,2,1,0:T(8,128)S(1)}, f32[4,7,7,128]{3,2,1,0:T(8,128)S(1)}) custom-call(bf16[16,16,128]{2,1,0:T(8,128)(2,1)S(1)} %copy-done, bf16[16,16,128]{2,1,0:T(8,128)(2,1)S(1)} %copy-done.1, f32[4,7,7,128]{3,2,1,0:T(8,128)S(1)} %copy.9.master, ...), custom_call_target="tpu_custom_call" | custom-call | tf_op jit(solution)/shard_map/dictionary_step/pallas_call | solution.py:294
  61.5 0.7 %copy.12 = f32[4,7,7,128]{3,0,2,1:T(4,128)} copy(f32[4,7,7,128]{3,2,1,0:T(8,128)S(1)} %get-tuple-element.5) | data formatting | bytes 200704 | tf_op jit(solution)/shard_map/dictionary_step/pallas_call | solution.py:294
  62.2 0.7 %copy.13 = f32[4,7,7,128]{3,0,2,1:T(4,128)} copy(f32[4,7,7,128]{3,2,1,0:T(8,128)S(1)} %get-tuple-element.6) | data formatting | bytes 200704 | tf_op jit(solution)/shard_map/dictionary_step/pallas_call | solution.py:294
  62.8 0.7 %copy.14 = f32[4,7,7,128]{3,0,2,1:T(4,128)} copy(f32[4,7,7,128]{3,2,1,0:T(8,128)S(1)} %get-tuple-element.7) | data formatting | bytes 200704 | tf_op jit(solution)/shard_map/dictionary_step/pallas_call | solution.py:294
  63.5 0.6 copy.16
  (2 shorter events, 0.0 us)
Async XLA Ops:
  0.6 1.0 %copy-start.2 = (f32[4,7,7,128]{3,0,2,1:T(4,128)S(1)}, f32[4,7,7,128]{3,0,2,1:T(4,128)}, u32[]{:S(2)}) copy-start(f32[4,7,7,128]{3,0,2,1:T(4,128)} %param.8) | copy-start | bytes 301060
  1.6 0.9 %copy-start.3 = (f32[4,7,7,128]{3,0,2,1:T(4,128)S(1)}, f32[4,7,7,128]{3,0,2,1:T(4,128)}, u32[]{:S(2)}) copy-start(f32[4,7,7,128]{3,0,2,1:T(4,128)} %param.9) | copy-start | bytes 301060
  2.5 0.8 %copy-start = (bf16[16,16,128]{2,1,0:T(8,128)(2,1)S(1)}, bf16[16,16,128]{2,1,0:T(8,128)(2,1)}, u32[]{:S(2)}) copy-start(bf16[16,16,128]{2,1,0:T(8,128)(2,1)} %codes.1) | copy-start | bytes 196612
  2.5 0.9 %copy-start.1 = (bf16[16,16,128]{2,1,0:T(8,128)(2,1)S(1)}, bf16[16,16,128]{2,1,0:T(8,128)(2,1)}, u32[]{:S(2)}) copy-start(bf16[16,16,128]{2,1,0:T(8,128)(2,1)} %image.1) | copy-start | bytes 196612

commit v2 on v1

v2 whole, which is shorter than its diff:
```python
import functools

import jax
import jax.numpy as jnp
from jax import lax
from jax.experimental import pallas as pl
from jax.experimental.pallas import tpu as pltpu
from jax.sharding import PartitionSpec as P

MESH = pl.DeviceIdType.MESH
F32, BF16 = jnp.float32, jnp.bfloat16
first_fix = 0.9999734386011124
second_fix = 0.09520785288629038
ROWS, COLS, ATOMS = 8, 4, 16
TAPS = 7


def kernel(
    codes, image, master,
    out_codes, out_grad,
    x_buf, x7, f_buf, m_buf,
    img_in, img_out, img_got,
    pt, part_out, part_got,
    resid, edge_got, xrg, xrb,
    g_out, g_sum, g_got, p2, bk_out, bk_sum, bk_got,
    in_sem, f_send, f_recv, c_send, c_recv, i_send, i_recv,
    z_send, z_recv, p_send, p_recv, r_send, r_recv, e_send, e_recv,
    g_send, g_recv, b_send, b_recv,
):
    r = lax.axis_index("row")
    q = lax.axis_index("col")
    t = lax.axis_index("atom")
    pair, half = t // 2, lax.rem(t, 2)
    started = []

    def start(copy):
        copy.start()
        started.append(copy)
        return copy

    def remote(src, dst, send, recv, who):
        return pltpu.make_async_remote_copy(
            src_ref=src, dst_ref=dst, send_sem=send, recv_sem=recv,
            device_id=who, device_id_type=MESH,
        )

    def row_at(d):
        return lax.rem(r + d + 2 * ROWS, ROWS)

    def col_at(d):
        return lax.rem(q + d + 2 * COLS, COLS)

    def tile_cols(at):
        return pl.ds(pl.multiple_of(at * 16, 16), 16)

    in_m = pltpu.make_async_copy(master, m_buf, in_sem.at[0])
    in_c = pltpu.make_async_copy(codes, x_buf.at[pl.ds(3, 16), tile_cols(q)], in_sem.at[1])
    in_i = pltpu.make_async_copy(image.at[pl.ds(2 * pair, 2)], img_in, in_sem.at[2])
    for copy in (in_m, in_c, in_i):
        copy.start()

    barrier = pltpu.get_barrier_semaphore()
    peers = [{"row": row_at(d)} for d in (1, -1, 2, -2)]
    peers += [{"col": col_at(d)} for d in range(1, COLS)]
    peers += [{"atom": lax.rem(t + d, ATOMS)} for d in range(1, ATOMS)]
    for who in peers:
        pl.semaphore_signal(barrier, inc=1, device_id=who, device_id_type=MESH)

    in_m.wait()
    for b in range(TAPS):
        rows = [m_buf[a * TAPS + b] for a in range(TAPS)] + [jnp.zeros((4, 128), F32)]
        f_buf[r, :, b * 128 : (b + 1) * 128] = jnp.concatenate(rows, axis=0).astype(BF16)

    pl.semaphore_wait(barrier, len(peers))

    def side(way):
        return 1 if way == 0 else -1

    @functools.cache
    def f_hop(way, kind):
        step, sem = side(way), way * 4 + kind
        rows = pl.ds(16 * way, 16) if kind == 3 else slice(None)
        piece = f_buf.at[r if kind < 2 else row_at(-2 * step), rows]
        to = row_at(step if kind in (0, 2) else 2 * step)
        return remote(piece, piece, f_send.at[sem], f_recv.at[sem], {"row": to})

    first = (3, 11, 0, 19)
    count = (8, 8, 3, 3)

    @functools.cache
    def c_hop(way, s, c):
        step = side(way)
        piece = x_buf.at[pl.ds(first[c], count[c]), tile_cols(col_at(-step * (s - 1)))]
        sem = (way * 2 + s - 1) * 4 + c
        return remote(piece, piece, c_send.at[sem], c_recv.at[sem], {"col": col_at(step)})

    @functools.cache
    def z_hop(way):
        step = side(way)
        src = x_buf.at[pl.ds(16 if way == 0 else 3, 3), tile_cols(q)]
        dst = x_buf.at[pl.ds(0 if way == 0 else 19, 3), tile_cols(q)]
        return remote(src, dst, z_send.at[way], z_recv.at[way], {"row": row_at(step)})

    def chunk(way, k):
        return k if way == 0 else 1 - k

    for way in range(2):
        start(f_hop(way, 1))
    in_c.wait()
    for way in range(2):
        start(z_hop(way))
    for way in range(2):
        start(f_hop(way, 0))
    for k in range(2):
        for way in range(2):
            start(c_hop(way, 1, chunk(way, k)))

    in_i.wait()
    n = lax.broadcasted_iota(jnp.int32, (64, 128), 0)
    lane = lax.broadcasted_iota(jnp.int32, (64, 128), 1)
    band = (4 * half + ((n >> 2) & 3)) * 16 + (n >> 4) * 4 + (n & 3)
    pick = jnp.where(lane == band, 1.0, 0.0).astype(BF16)
    picked = lax.dot_general(
        pick, img_in[...].reshape(32, 128), (((1,), (1,)), ((), ())), preferred_element_type=F32
    ).astype(BF16)
    n = lax.broadcasted_iota(jnp.int32, (32, 128), 0)
    lane = lax.broadcasted_iota(jnp.int32, (32, 128), 1)
    place = jnp.where(lane == (n >> 4) * 64 + q * 16 + (n & 15), 1.0, 0.0).astype(BF16)
    img_out[...] = jnp.dot(picked, place, preferred_element_type=F32).astype(BF16).reshape(COLS, 16, 128)

    for way in range(2):
        z_hop(way).wait_recv()
    for way in range(2):
        for k in range(2):
            start(c_hop(way, 1, 2 + chunk(way, k)))
    for way in range(2):
        f_hop(way, 1).wait_recv()
        start(f_hop(way, 2))
        start(f_hop(way, 3))
    for way in range(2):
        c_hop(way, 1, way).wait_recv()
        start(c_hop(way, 2, way))
    for way in range(2):
        c_hop(way, 1, 2 + way).wait_recv()
        start(c_hop(way, 2, 2 + way))
    i_copies = []
    for d in range(1, COLS):
        to = col_at(d)
        i_copies.append(
            start(remote(img_out.at[to], img_got.at[d - 1], i_send.at[d - 1], i_recv.at[d - 1], {"col": to}))
        )

    v = lax.broadcasted_iota(jnp.int32, (64, 128), 0)

    def shift_codes(e, carry):
        x = x_buf[e].astype(F32)
        inside = ((e >= 3) | (r > 0)) & ((e < 19) | (r < ROWS - 1))
        x = jnp.where(inside, x, 0.0)
        for b in range(TAPS):
            s = b - 3
            moved = x if s == 0 else pltpu.roll(x, (-s) % 64, 0)
            if s:
                moved = jnp.where((v + s >= 0) & (v + s < 64), moved, 0.0)
            x7[pl.ds(pl.multiple_of(e * 64, 64), 64), b * 128 : (b + 1) * 128] = moved.astype(BF16)
        return carry

    for way in range(2):
        c_hop(way, 1, 1 - way).wait_recv()
        c_hop(way, 1, 3 - way).wait_recv()
    c_hop(0, 2, 0).wait_recv()
    lax.fori_loop(3, 11, shift_codes, 0)
    c_hop(1, 2, 1).wait_recv()
    lax.fori_loop(11, 19, shift_codes, 0)
    c_hop(0, 2, 2).wait_recv()
    lax.fori_loop(0, 3, shift_codes, 0)
    c_hop(1, 2, 3).wait_recv()
    lax.fori_loop(19, 22, shift_codes, 0)
    for way in range(2):
        for kind in (0, 2, 3):
            f_hop(way, kind).wait_recv()

    product = lax.dot_general(
        f_buf[...].reshape(256, 896), x7[...], (((1,), (1,)), ((), ())), preferred_element_type=F32
    )
    pt[...] = product.reshape(8, 4, 8, 1408)

    lane = lax.broadcasted_iota(jnp.int32, (32, 128), 1)
    low = lax.broadcasted_iota(jnp.int32, (4, 8, 128), 1) < 4

    def swapped(x):
        return pltpu.roll(x, 64, 1)

    def turned(x):
        return pltpu.roll(x, 4, 1)

    def tap_sums(j):
        total = None
        for m in range(4):
            if j + m < 11:
                term = pt[:, m, :, (j + m) * 128 : (j + m + 1) * 128]
                total = term if total is None else total + term
        total = total.reshape(4, 2, 8, 128)
        one, two = total[:, 0], total[:, 1]
        even = jnp.where(low, one, turned(two)).reshape(32, 128)
        odd = jnp.where(low, turned(one), two).reshape(32, 128)
        return even, swapped(odd)

    even, odd = tap_sums(0)
    for p in range(8):
        next_even, next_odd = tap_sums(p + 1)
        value = even + jnp.where(lane < 64, odd, next_odd)
        part_out[2 * p] = value[:16].astype(BF16)
        part_out[2 * p + 1] = value[16:].astype(BF16)
        even, odd = next_even, next_odd
    p_copies = []
    for d in range(1, ATOMS):
        to = lax.rem(t + d, ATOMS)
        p_copies.append(
            start(remote(part_out.at[to], part_got.at[d - 1], p_send.at[d - 1], p_recv.at[d - 1], {"atom": to}))
        )
    for copy in i_copies:
        copy.wait_recv()
    own_image = img_out[q].astype(F32)
    for d in range(COLS - 1):
        own_image = own_image + img_got[d].astype(F32)
    synth = part_out[t].astype(F32)
    for copy in p_copies:
        copy.wait_recv()
    for d in range(ATOMS - 1):
        synth = synth + part_got[d].astype(F32)
    resid[t] = (synth - own_image).astype(BF16)
    r_copies = []
    for d in range(1, ATOMS):
        to = lax.rem(t + d, ATOMS)
        r_copies.append(
            start(remote(resid.at[t], resid.at[t], r_send.at[d - 1], r_recv.at[d - 1], {"atom": to}))
        )
    for copy in r_copies:
        copy.wait_recv()
    e_copies = [
        start(remote(resid.at[pl.ds(0, 4)], edge_got.at[1], e_send.at[0], e_recv.at[0], {"row": row_at(-1)})),
        start(remote(resid.at[pl.ds(12, 4)], edge_got.at[0], e_send.at[1], e_recv.at[1], {"row": row_at(1)})),
    ]

    def tile_of(ref, p):
        return jnp.concatenate([ref[2 * p], ref[2 * p + 1]], axis=0).astype(F32)

    tiles = {2 + p: tile_of(resid, p) for p in range(8)}
    flipped = {j: swapped(tiles[j]) for j in range(2, 10)}
    zero = jnp.zeros((32, 128), F32)

    def paired(even, odd):
        even, odd = even.reshape(4, 8, 128), odd.reshape(4, 8, 128)
        one, two = jnp.where(low, even, turned(odd)), jnp.where(low, turned(even), odd)
        return jnp.stack([one, two], axis=1).reshape(8, 8, 128)

    shares = [
        paired(tiles.get(j + 2, zero), jnp.where(lane < 64, flipped.get(j + 1, zero), flipped.get(j + 2, zero)))
        if j < 8 else paired(zero, jnp.where(lane < 64, flipped[9], zero))
        for j in range(9)
    ]
    none = jnp.zeros((8, 8, 128), F32)
    for j in range(11):
        taps = [shares[j - m] if 0 <= j - m < 9 else none for m in range(4)]
        xrg[:, j * 128 : (j + 1) * 128] = jnp.stack(taps, axis=1).reshape(256, 128).astype(BF16)

    grad = jnp.dot(xrg[...], x7[...], preferred_element_type=F32)
    g_out[...] = grad.astype(BF16).reshape(ROWS, 32, 896)

    @functools.cache
    def g_hop(way, kind):
        step, sem = side(way), way * 4 + kind
        rows = pl.ds(16 * way, 16) if kind == 1 else slice(None)
        src = g_sum.at[way] if kind == 3 else g_out.at[row_at(step * (3, 4, 1)[kind]), rows]
        to = row_at(step if kind in (0, 2) else 2 * step)
        return remote(src, g_got.at[way, kind, rows], g_send.at[sem], g_recv.at[sem], {"row": to})

    def g_relay():
        for way in range(2):
            g_hop(way, 0).wait_recv()
            g_hop(way, 1).wait_recv()
            dest = row_at(2 * side(way))
            term = g_out[dest].astype(F32) + g_got[way, 0].astype(F32)
            near = slice(16 * way, 16 * way + 16)
            far = slice(16 - 16 * way, 32 - 16 * way)
            g_sum[way, near, :] = (term[near] + g_got[way, 1, near, :].astype(F32)).astype(BF16)
            g_sum[way, far, :] = term[far].astype(BF16)
            start(g_hop(way, 3))

    for kind in range(3):
        for way in range(2):
            start(g_hop(way, kind))

    not_first = jnp.where(r > 0, 1.0, 0.0).astype(F32)
    not_last = jnp.where(r < ROWS - 1, 1.0, 0.0).astype(F32)
    for copy in e_copies:
        copy.wait_recv()
    for at in range(2):
        tiles[at] = not_first * tile_of(edge_got.at[0], at)
        tiles[10 + at] = not_last * tile_of(edge_got.at[1], at)
        flipped[at] = swapped(tiles[at])
        flipped[10 + at] = swapped(tiles[10 + at])
    both = [paired(jnp.where(lane < 64, flipped[j], flipped[j + 1]), tiles[j]) for j in range(11)]
    for j in range(8):
        tap_rows = jnp.stack([both[j + 3 - m] for m in range(4)], axis=1).reshape(256, 128)
        xrb[:, j * 128 : (j + 1) * 128] = tap_rows.astype(BF16)

    def back_part(at):
        cols = slice(at * 512, (at + 1) * 512)
        p2[...] = lax.dot_general(
            xrb[:, cols], f_buf[...].reshape(256, 896), (((0,), (0,)), ((), ())), preferred_element_type=F32
        )

        def shift_back(u, carry):
            here = pl.ds(pl.multiple_of(u * 64, 64), 64)
            total = p2[here, 384:512]
            for b in range(TAPS):
                s = b - 3
                if s:
                    moved = pltpu.roll(p2[here, b * 128 : (b + 1) * 128], s % 64, 0)
                    total = total + jnp.where((v - s >= 0) & (v - s < 64), moved, 0.0)
            bk_out[at * 8 + u] = total.astype(BF16)
            return carry

        lax.fori_loop(0, 8, shift_back, 0)

    @functools.cache
    def b_hop(way, s, c):
        step = side(way)
        rows = pl.ds(8 * c, 8)
        alone = s == 2 or c == chunk(way, 1)
        src = bk_out.at[rows, tile_cols(col_at(step * s))] if alone else bk_sum.at[way]
        sem = (way * 2 + s - 1) * 2 + c
        return remote(src, bk_got.at[way, s - 1, rows], b_send.at[sem], b_recv.at[sem], {"col": col_at(step)})

    def b_step(way):
        c = chunk(way, 0)
        b_hop(way, 2, c).wait_recv()
        own = bk_out[8 * c : 8 * c + 8, tile_cols(col_at(1 if way == 0 else -1)), :].astype(F32)
        bk_sum[way] = (own + bk_got[way, 1, 8 * c : 8 * c + 8].astype(F32)).astype(BF16)
        start(b_hop(way, 1, c))

    back_part(0)
    start(b_hop(0, 2, 0))
    start(b_hop(1, 1, 0))
    g_relay()
    back_part(1)
    start(b_hop(1, 2, 1))
    start(b_hop(0, 1, 1))
    b_step(0)
    b_step(1)
    for way in range(2):
        for c in range(2):
            b_hop(way, 1, c).wait_recv()

    def shrink(u, carry):
        back = bk_out[u, tile_cols(q)].astype(F32)
        for way in range(2):
            back = back + bk_got[way, 0, u].astype(F32)
        moved = x_buf[u + 3, tile_cols(q)].astype(F32) - 0.05 * back
        out_codes[u] = (moved - jnp.clip(moved, -0.02, 0.02)).astype(BF16)
        return carry

    lax.fori_loop(0, 16, shrink, 0)

    for way in range(2):
        for kind in (2, 3):
            g_hop(way, kind).wait_recv()
    for b in range(TAPS):
        cols = slice(b * 128, (b + 1) * 128)
        total = g_out[r, :, cols].astype(F32)
        for way in range(2):
            for kind in (2, 3):
                total = total + g_got[way, kind, :, cols].astype(F32)
        for a in range(TAPS):
            out_grad[a * TAPS + b] = total[4 * a : 4 * a + 4]

    for copy in started:
        copy.wait_send()


def adam_update(master, moment, second, grad):
    new_moment = 0.9 * moment + 0.1 * grad
    new_second = 0.999 * second + 0.001 * grad * grad
    new_dictionary = master - 0.05 * (new_moment / first_fix) / (
        jnp.sqrt(new_second / second_fix) + 1e-08
    )
    return (new_dictionary, new_moment, new_second)


def local(codes, image, master, moment, second):
    dma = pltpu.SemaphoreType.DMA
    vmem = pltpu.VMEM
    hbm_spec = pl.BlockSpec(memory_space=pltpu.HBM)
    vmem_spec = pl.BlockSpec(memory_space=vmem)
    bands = master.shape[0]
    taps = TAPS * TAPS
    new_codes, grad = pl.pallas_call(
        kernel,
        out_shape=(
            jax.ShapeDtypeStruct(codes.shape, BF16),
            jax.ShapeDtypeStruct((taps, bands, 128), F32),
        ),
        in_specs=[hbm_spec] * 3,
        out_specs=(vmem_spec,) * 2,
        scratch_shapes=[
            vmem((22, 64, 128), BF16),
            vmem((1408, 896), BF16),
            vmem((8, 32, 896), BF16),
            vmem((taps, bands, 128), F32),
            vmem((2, 16, 128), BF16),
            vmem((4, 16, 128), BF16),
            vmem((3, 16, 128), BF16),
            vmem((8, 4, 8, 1408), F32),
            vmem((16, 16, 128), BF16),
            vmem((15, 16, 128), BF16),
            vmem((16, 16, 128), BF16),
            vmem((2, 4, 16, 128), BF16),
            vmem((256, 1408), BF16),
            vmem((256, 1024), BF16),
            vmem((8, 32, 896), BF16),
            vmem((2, 32, 896), BF16),
            vmem((2, 4, 32, 896), BF16),
            vmem((512, 896), F32),
            vmem((16, 64, 128), BF16),
            vmem((2, 8, 16, 128), BF16),
            vmem((2, 2, 16, 16, 128), BF16),
            dma((3,)),
            dma((8,)), dma((8,)), dma((16,)), dma((16,)), dma((3,)), dma((3,)),
            dma((2,)), dma((2,)), dma((15,)), dma((15,)), dma((15,)), dma((15,)), dma((2,)), dma((2,)),
            dma((8,)), dma((8,)), dma((8,)), dma((8,)),
        ],
        compiler_params=pltpu.CompilerParams(
            collective_id=0, has_side_effects=True, vmem_limit_bytes=60 * 1024 * 1024
        ),
        name="dictionary_step",
    )(codes, image, jnp.transpose(master, (1, 2, 0, 3)).reshape(taps, bands, 128))
    grad = jnp.transpose(grad.reshape(TAPS, TAPS, bands, 128), (2, 0, 1, 3))
    return (new_codes, *adam_update(master, moment, second, grad))


def solution(mesh):
    tile = P("row", "col", "atom")
    bank = P(("row", "col"), None, None, "atom")
    return jax.shard_map(
        local,
        mesh=mesh,
        in_specs=(tile, P("row", "col", None), bank, bank, bank),
        out_specs=(tile, bank, bank, bank),
        check_vma=False,
    )
```

time: 64.4 us -> 56.1 us (0.87)
  the two profiles are of different devices: /device:TPU:1 before, /device:TPU:64 now
where the time goes in v2:
time: 56.1 us; the launch traced here: 55.9 us
  Pallas kernels  52.8 us (94%)
  other arithmetic  1.8 us (3%)
  between operations  0.68 us (1%)
  local copies, waits for them, and re-layouts  0.64 us (1%)
    pallas_call x1, Pallas kernels, local(): pl.pallas_call(kernel, out_shape=(jax.ShapeDtypeStruct(codes.shape, BF16)...  52.8 us
    sub x1, other arithmetic, adam_update(): master - 0.05 * (new_moment / first_fix) / (jnp.sqrt(new_second / second_...  1.8 us

profile of v2, /device:TPU:64, one launch (start us, length us, event | category | flops | bytes accessed | tf_op | source)
XLA Modules:
  0.0 55.9 jit_solution(16246015696489545969)
XLA Ops:
  0.6 0.0 copy-start
  0.6 0.0 copy-start.1
  0.7 52.8 %dictionary_step.1 = (bf16[16,16,128]{2,1,0:T(8,128)(2,1)}, f32[49,4,128]{2,1,0:T(4,128)}) custom-call(bf16[16,16,128]{2,1,0:T(8,128)(2,1)} %codes.1, bf16[16,16,128]{2,1,0:T(8,128)(2,1)} %image.1, f32[49,4,128]{2,1,0:T(4,128)} %bitcast.6), custom_call_target="tpu_custom_call" | custom-call | tf_op jit(solution)/shard_map/dictionary_step/pallas_call | solution.py:398
  53.4 0.0 copy-done
  53.4 0.0 copy-done.1
  53.4 0.0 copy-start.2
  53.4 1.8 %divide_subtract_fusion = (f32[4,7,7,128]{3,0,2,1:T(4,128)}, f32[4,7,7,128]{3,0,2,1:T(4,128)}, f32[4,7,7,128]{3,0,2,1:T(4,128)}) fusion(f32[4,7,7,128]{3,0,2,1:T(4,128)S(1)} %copy-done, f32[4,7,7,128]{3,0,2,1:T(4,128)} %bitcast.7, f32[4,7,7,128]{3,0,2,1:T(4,128)S(1)} %copy-done.1, f32[4,7,7,128]{3,0,2,1:T(4,128)} %param.9), kind=kLoop, calls=%fused_computation.2 | loop fusion | flops 301056 | bytes 702464 | tf_op jit(solution)/shard_map/sub | solution.py:385
  55.3 0.0 copy-done.2
  55.3 0.6 %copy.10 = bf16[16,16,128]{2,1,0:T(8,128)(2,1)} copy(bf16[16,16,128]{2,1,0:T(8,128)(2,1)S(1)} %copy-done.2) | data formatting | bytes 131072
Async XLA Ops:
  0.6 52.8 %copy-start = (f32[4,7,7,128]{3,0,2,1:T(4,128)S(1)}, f32[4,7,7,128]{3,0,2,1:T(4,128)}, u32[]{:S(2)}) copy-start(f32[4,7,7,128]{3,0,2,1:T(4,128)} %param.7) | copy-start | bytes 301060
  0.6 52.8 %copy-start.1 = (f32[4,7,7,128]{3,0,2,1:T(4,128)S(1)}, f32[4,7,7,128]{3,0,2,1:T(4,128)}, u32[]{:S(2)}) copy-start(f32[4,7,7,128]{3,0,2,1:T(4,128)} %param.8) | copy-start | bytes 301060
  53.4 1.8 %copy-start.2 = (bf16[16,16,128]{2,1,0:T(8,128)(2,1)S(1)}, bf16[16,16,128]{2,1,0:T(8,128)(2,1)}, u32[]{:S(2)}) copy-start(bf16[16,16,128]{2,1,0:T(8,128)(2,1)} %get-tuple-element.15) | copy-start | bytes 196612

commit v3 on v2

--- a/solution.py
+++ b/solution.py
@@ -18,13 +18,13 @@
 def kernel(
     codes, image, master,
     out_codes, out_grad,
-    x_buf, x7, f_buf, m_buf,
+    x_buf, x_edge, x7, f_buf, m_buf,
     img_in, img_out, img_got,
     pt, part_out, part_got,
     resid, edge_got, xrg, xrb,
     g_out, g_sum, g_got, p2, bk_out, bk_sum, bk_got,
     in_sem, f_send, f_recv, c_send, c_recv, i_send, i_recv,
-    z_send, z_recv, p_send, p_recv, r_send, r_recv, e_send, e_recv,
+    z_send, z_recv, h_send, h_recv, p_send, p_recv, r_send, r_recv, e_send, e_recv,
     g_send, g_recv, b_send, b_recv,
 ):
     r = lax.axis_index("row")
@@ -54,7 +54,7 @@
         return pl.ds(pl.multiple_of(at * 16, 16), 16)
 
     in_m = pltpu.make_async_copy(master, m_buf, in_sem.at[0])
-    in_c = pltpu.make_async_copy(codes, x_buf.at[pl.ds(3, 16), tile_cols(q)], in_sem.at[1])
+    in_c = pltpu.make_async_copy(codes, x_buf.at[:, tile_cols(q)], in_sem.at[1])
     in_i = pltpu.make_async_copy(image.at[pl.ds(2 * pair, 2)], img_in, in_sem.at[2])
     for copy in (in_m, in_c, in_i):
         copy.start()
@@ -84,22 +84,23 @@
         to = row_at(step if kind in (0, 2) else 2 * step)
         return remote(piece, piece, f_send.at[sem], f_recv.at[sem], {"row": to})
 
-    first = (3, 11, 0, 19)
-    count = (8, 8, 3, 3)
-
     @functools.cache
     def c_hop(way, s, c):
         step = side(way)
-        piece = x_buf.at[pl.ds(first[c], count[c]), tile_cols(col_at(-step * (s - 1)))]
-        sem = (way * 2 + s - 1) * 4 + c
+        piece = x_buf.at[pl.ds(8 * c, 8), tile_cols(col_at(-step * (s - 1)))]
+        sem = (way * 2 + s - 1) * 2 + c
         return remote(piece, piece, c_send.at[sem], c_recv.at[sem], {"col": col_at(step)})
 
     @functools.cache
     def z_hop(way):
-        step = side(way)
-        src = x_buf.at[pl.ds(16 if way == 0 else 3, 3), tile_cols(q)]
-        dst = x_buf.at[pl.ds(0 if way == 0 else 19, 3), tile_cols(q)]
-        return remote(src, dst, z_send.at[way], z_recv.at[way], {"row": row_at(step)})
+        src = x_buf.at[pl.ds(13 if way == 0 else 0, 3), tile_cols(q)]
+        dst = x_edge.at[pl.ds(3 * way, 3), tile_cols(q)]
+        return remote(src, dst, z_send.at[way], z_recv.at[way], {"row": row_at(side(way))})
+
+    @functools.cache
+    def h_hop(d):
+        piece = x_edge.at[:, tile_cols(q)]
+        return remote(piece, piece, h_send.at[d - 1], h_recv.at[d - 1], {"col": col_at(d)})
 
     def chunk(way, k):
         return k if way == 0 else 1 - k
@@ -130,9 +131,8 @@
 
     for way in range(2):
         z_hop(way).wait_recv()
-    for way in range(2):
-        for k in range(2):
-            start(c_hop(way, 1, 2 + chunk(way, k)))
+    for d in (1, 3, 2):
+        start(h_hop(d))
     for way in range(2):
         f_hop(way, 1).wait_recv()
         start(f_hop(way, 2))
@@ -140,9 +140,6 @@
     for way in range(2):
         c_hop(way, 1, way).wait_recv()
         start(c_hop(way, 2, way))
-    for way in range(2):
-        c_hop(way, 1, 2 + way).wait_recv()
-        start(c_hop(way, 2, 2 + way))
     i_copies = []
     for d in range(1, COLS):
         to = col_at(d)
@@ -152,29 +149,34 @@
 
     v = lax.broadcasted_iota(jnp.int32, (64, 128), 0)
 
-    def shift_codes(e, carry):
-        x = x_buf[e].astype(F32)
-        inside = ((e >= 3) | (r > 0)) & ((e < 19) | (r < ROWS - 1))
-        x = jnp.where(inside, x, 0.0)
+    def shift_codes(x, at):
+        x = x.astype(F32)
         for b in range(TAPS):
             s = b - 3
             moved = x if s == 0 else pltpu.roll(x, (-s) % 64, 0)
             if s:
                 moved = jnp.where((v + s >= 0) & (v + s < 64), moved, 0.0)
-            x7[pl.ds(pl.multiple_of(e * 64, 64), 64), b * 128 : (b + 1) * 128] = moved.astype(BF16)
+            x7[pl.ds(pl.multiple_of(at * 64, 64), 64), b * 128 : (b + 1) * 128] = moved.astype(BF16)
+
+    def shift_tile(u, carry):
+        shift_codes(x_buf[u], u + 3)
         return carry
 
+    def shift_edge(e, carry):
+        x = x_edge[e]
+        inside = jnp.where(e < 3, r, ROWS - 1 - r) > 0
+        shift_codes(jnp.where(inside, x, jnp.zeros_like(x)), jnp.where(e < 3, e, e + 16))
+        return carry
+
+    for d in range(1, COLS):
+        h_hop(d).wait_recv()
+    lax.fori_loop(0, 6, shift_edge, 0)
     for way in range(2):
         c_hop(way, 1, 1 - way).wait_recv()
-        c_hop(way, 1, 3 - way).wait_recv()
     c_hop(0, 2, 0).wait_recv()
-    lax.fori_loop(3, 11, shift_codes, 0)
+    lax.fori_loop(0, 8, shift_tile, 0)
     c_hop(1, 2, 1).wait_recv()
-    lax.fori_loop(11, 19, shift_codes, 0)
-    c_hop(0, 2, 2).wait_recv()
-    lax.fori_loop(0, 3, shift_codes, 0)
-    c_hop(1, 2, 3).wait_recv()
-    lax.fori_loop(19, 22, shift_codes, 0)
+    lax.fori_loop(8, 16, shift_tile, 0)
     for way in range(2):
         for kind in (0, 2, 3):
             f_hop(way, kind).wait_recv()
@@ -291,19 +293,17 @@
         for way in range(2):
             start(g_hop(way, kind))
 
-    not_first = jnp.where(r > 0, 1.0, 0.0).astype(F32)
-    not_last = jnp.where(r < ROWS - 1, 1.0, 0.0).astype(F32)
-    for copy in e_copies:
-        copy.wait_recv()
-    for at in range(2):
-        tiles[at] = not_first * tile_of(edge_got.at[0], at)
-        tiles[10 + at] = not_last * tile_of(edge_got.at[1], at)
-        flipped[at] = swapped(tiles[at])
-        flipped[10 + at] = swapped(tiles[10 + at])
-    both = [paired(jnp.where(lane < 64, flipped[j], flipped[j + 1]), tiles[j]) for j in range(11)]
-    for j in range(8):
+    both = {}
+
+    def rows_of_taps(slot, j):
+        for at in range(j, j + 4):
+            if at not in both:
+                both[at] = paired(jnp.where(lane < 64, flipped[at], flipped[at + 1]), tiles[at])
         tap_rows = jnp.stack([both[j + 3 - m] for m in range(4)], axis=1).reshape(256, 128)
-        xrb[:, j * 128 : (j + 1) * 128] = tap_rows.astype(BF16)
+        xrb[:, slot * 128 : (slot + 1) * 128] = tap_rows.astype(BF16)
+
+    for slot in range(4):
+        rows_of_taps(slot, slot + 2)
 
     def back_part(at):
         cols = slice(at * 512, (at + 1) * 512)
@@ -343,21 +343,33 @@
     back_part(0)
     start(b_hop(0, 2, 0))
     start(b_hop(1, 1, 0))
-    g_relay()
+    not_first = jnp.where(r > 0, 1.0, 0.0).astype(F32)
+    not_last = jnp.where(r < ROWS - 1, 1.0, 0.0).astype(F32)
+    for copy in e_copies:
+        copy.wait_recv()
+    for at in range(2):
+        tiles[at] = not_first * tile_of(edge_got.at[0], at)
+        tiles[10 + at] = not_last * tile_of(edge_got.at[1], at)
+        flipped[at] = swapped(tiles[at])
+        flipped[10 + at] = swapped(tiles[10 + at])
+    for slot, j in enumerate((0, 1, 6, 7)):
+        rows_of_taps(4 + slot, j)
     back_part(1)
     start(b_hop(1, 2, 1))
     start(b_hop(0, 1, 1))
+    g_relay()
     b_step(0)
     b_step(1)
     for way in range(2):
         for c in range(2):
             b_hop(way, 1, c).wait_recv()
 
-    def shrink(u, carry):
-        back = bk_out[u, tile_cols(q)].astype(F32)
+    def shrink(at, carry):
+        u = jnp.where(at < 8, at + 4, jnp.where(at < 12, at - 8, at))
+        back = bk_out[at, tile_cols(q)].astype(F32)
         for way in range(2):
-            back = back + bk_got[way, 0, u].astype(F32)
-        moved = x_buf[u + 3, tile_cols(q)].astype(F32) - 0.05 * back
+            back = back + bk_got[way, 0, at].astype(F32)
+        moved = x_buf[u, tile_cols(q)].astype(F32) - 0.05 * back
         out_codes[u] = (moved - jnp.clip(moved, -0.02, 0.02)).astype(BF16)
         return carry
 
@@ -404,7 +416,8 @@
         in_specs=[hbm_spec] * 3,
         out_specs=(vmem_spec,) * 2,
         scratch_shapes=[
-            vmem((22, 64, 128), BF16),
+            vmem((16, 64, 128), BF16),
+            vmem((6, 64, 128), BF16),
             vmem((1408, 896), BF16),
             vmem((8, 32, 896), BF16),
             vmem((taps, bands, 128), F32),
@@ -426,8 +439,8 @@
             vmem((2, 8, 16, 128), BF16),
             vmem((2, 2, 16, 16, 128), BF16),
             dma((3,)),
-            dma((8,)), dma((8,)), dma((16,)), dma((16,)), dma((3,)), dma((3,)),
-            dma((2,)), dma((2,)), dma((15,)), dma((15,)), dma((15,)), dma((15,)), dma((2,)), dma((2,)),
+            dma((8,)), dma((8,)), dma((8,)), dma((8,)), dma((3,)), dma((3,)),
+            dma((2,)), dma((2,)), dma((3,)), dma((3,)), dma((15,)), dma((15,)), dma((15,)), dma((15,)), dma((2,)), dma((2,)),
             dma((8,)), dma((8,)), dma((8,)), dma((8,)),
         ],
         compiler_params=pltpu.CompilerParams(

time: 56.1 us -> 52.6 us (0.938)
  the two profiles are of different devices: /device:TPU:64 before, /device:TPU:1 now
where the time goes in v3:
time: 52.6 us; the launch traced here: 52.4 us
  Pallas kernels  49.3 us (94%)
  other arithmetic  1.8 us (3%)
  between operations  0.68 us (1%)
  local copies, waits for them, and re-layouts  0.64 us (1%)
    pallas_call x1, Pallas kernels, local(): pl.pallas_call(kernel, out_shape=(jax.ShapeDtypeStruct(codes.shape, BF16)...  49.3 us
    sub x1, other arithmetic, adam_update(): master - 0.05 * (new_moment / first_fix) / (jnp.sqrt(new_second / second_...  1.8 us

profile of v3, /device:TPU:1, one launch (start us, length us, event | category | flops | bytes accessed | tf_op | source)
XLA Modules:
  0.0 52.4 jit_solution(17759488944435788981)
XLA Ops:
  0.6 0.0 copy-start
  0.6 0.0 copy-start.1
  0.7 49.3 %dictionary_step.1 = (bf16[16,16,128]{2,1,0:T(8,128)(2,1)}, f32[49,4,128]{2,1,0:T(4,128)}) custom-call(bf16[16,16,128]{2,1,0:T(8,128)(2,1)} %codes.1, bf16[16,16,128]{2,1,0:T(8,128)(2,1)} %image.1, f32[49,4,128]{2,1,0:T(4,128)} %bitcast.6), custom_call_target="tpu_custom_call" | custom-call | tf_op jit(solution)/shard_map/dictionary_step/pallas_call | solution.py:410
  50.0 0.0 copy-done
  50.0 0.0 copy-done.1
  50.0 0.0 copy-start.2
  50.0 1.8 %divide_subtract_fusion = (f32[4,7,7,128]{3,0,2,1:T(4,128)}, f32[4,7,7,128]{3,0,2,1:T(4,128)}, f32[4,7,7,128]{3,0,2,1:T(4,128)}) fusion(f32[4,7,7,128]{3,0,2,1:T(4,128)S(1)} %copy-done, f32[4,7,7,128]{3,0,2,1:T(4,128)} %bitcast.7, f32[4,7,7,128]{3,0,2,1:T(4,128)S(1)} %copy-done.1, f32[4,7,7,128]{3,0,2,1:T(4,128)} %param.9), kind=kLoop, calls=%fused_computation.2 | loop fusion | flops 301056 | bytes 702464 | tf_op jit(solution)/shard_map/sub | solution.py:397
  51.8 0.0 copy-done.2
  51.8 0.6 %copy.10 = bf16[16,16,128]{2,1,0:T(8,128)(2,1)} copy(bf16[16,16,128]{2,1,0:T(8,128)(2,1)S(1)} %copy-done.2) | data formatting | bytes 131072
Async XLA Ops:
  0.6 49.3 %copy-start = (f32[4,7,7,128]{3,0,2,1:T(4,128)S(1)}, f32[4,7,7,128]{3,0,2,1:T(4,128)}, u32[]{:S(2)}) copy-start(f32[4,7,7,128]{3,0,2,1:T(4,128)} %param.7) | copy-start | bytes 301060
  0.6 49.3 %copy-start.1 = (f32[4,7,7,128]{3,0,2,1:T(4,128)S(1)}, f32[4,7,7,128]{3,0,2,1:T(4,128)}, u32[]{:S(2)}) copy-start(f32[4,7,7,128]{3,0,2,1:T(4,128)} %param.8) | copy-start | bytes 301060
  50.0 1.8 %copy-start.2 = (bf16[16,16,128]{2,1,0:T(8,128)(2,1)S(1)}, bf16[16,16,128]{2,1,0:T(8,128)(2,1)}, u32[]{:S(2)}) copy-start(bf16[16,16,128]{2,1,0:T(8,128)(2,1)} %get-tuple-element.15) | copy-start | bytes 196612

commit v4 on v3

--- a/solution.py
+++ b/solution.py
@@ -105,16 +105,14 @@
     def chunk(way, k):
         return k if way == 0 else 1 - k
 
-    for way in range(2):
+    in_c.wait()
+    for way in range(2):
+        start(c_hop(way, 1, way))
         start(f_hop(way, 1))
-    in_c.wait()
     for way in range(2):
         start(z_hop(way))
     for way in range(2):
-        start(f_hop(way, 0))
-    for k in range(2):
-        for way in range(2):
-            start(c_hop(way, 1, chunk(way, k)))
+        start(c_hop(way, 1, 1 - way))
 
     in_i.wait()
     n = lax.broadcasted_iota(jnp.int32, (64, 128), 0)
@@ -134,19 +132,14 @@
     for d in (1, 3, 2):
         start(h_hop(d))
     for way in range(2):
-        f_hop(way, 1).wait_recv()
-        start(f_hop(way, 2))
-        start(f_hop(way, 3))
-    for way in range(2):
         c_hop(way, 1, way).wait_recv()
         start(c_hop(way, 2, way))
-    i_copies = []
-    for d in range(1, COLS):
-        to = col_at(d)
-        i_copies.append(
-            start(remote(img_out.at[to], img_got.at[d - 1], i_send.at[d - 1], i_recv.at[d - 1], {"col": to}))
-        )
-
+    for way in range(2):
+        f_hop(way, 1).wait_recv()
+        start(f_hop(way, 3))
+        start(f_hop(way, 2))
+    for way in range(2):
+        start(f_hop(way, 0))
     v = lax.broadcasted_iota(jnp.int32, (64, 128), 0)
 
     def shift_codes(x, at):
@@ -180,6 +173,13 @@
     for way in range(2):
         for kind in (0, 2, 3):
             f_hop(way, kind).wait_recv()
+
+    i_copies = []
+    for d in range(1, COLS):
+        to = col_at(d)
+        i_copies.append(
+            start(remote(img_out.at[to], img_got.at[d - 1], i_send.at[d - 1], i_recv.at[d - 1], {"col": to}))
+        )
 
     product = lax.dot_general(
         f_buf[...].reshape(256, 896), x7[...], (((1,), (1,)), ((), ())), preferred_element_type=F32
@@ -289,7 +289,7 @@
             g_sum[way, far, :] = term[far].astype(BF16)
             start(g_hop(way, 3))
 
-    for kind in range(3):
+    for kind in range(2):
         for way in range(2):
             start(g_hop(way, kind))
 
@@ -358,6 +358,8 @@
     start(b_hop(1, 2, 1))
     start(b_hop(0, 1, 1))
     g_relay()
+    for way in range(2):
+        start(g_hop(way, 2))
     b_step(0)
     b_step(1)
     for way in range(2):

time: 52.6 us -> 52.1 us (level)
  no operation moved by 1% of the time
where the time goes in v4:
time: 52.1 us; the launch traced here: 52 us
  Pallas kernels  48.8 us (94%)
  other arithmetic  1.8 us (3%)
  between operations  0.68 us (1%)
  local copies, waits for them, and re-layouts  0.64 us (1%)
    pallas_call x1, Pallas kernels, local(): pl.pallas_call(kernel, out_shape=(jax.ShapeDtypeStruct(codes.shape, BF16)...  48.8 us
    sub x1, other arithmetic, adam_update(): master - 0.05 * (new_moment / first_fix) / (jnp.sqrt(new_second / second_...  1.8 us

profile of v4, /device:TPU:1, one launch (start us, length us, event | category | flops | bytes accessed | tf_op | source)
XLA Modules:
  0.0 52.0 jit_solution(16594448590940293801)
XLA Ops:
  0.6 0.0 copy-start
  0.6 0.0 copy-start.1
  0.7 48.8 %dictionary_step.1 = (bf16[16,16,128]{2,1,0:T(8,128)(2,1)}, f32[49,4,128]{2,1,0:T(4,128)}) custom-call(bf16[16,16,128]{2,1,0:T(8,128)(2,1)} %codes.1, bf16[16,16,128]{2,1,0:T(8,128)(2,1)} %image.1, f32[49,4,128]{2,1,0:T(4,128)} %bitcast.6), custom_call_target="tpu_custom_call" | custom-call | tf_op jit(solution)/shard_map/dictionary_step/pallas_call | solution.py:412
  49.5 0.0 copy-done
  49.5 0.0 copy-done.1
  49.5 0.0 copy-start.2
  49.5 1.8 %divide_subtract_fusion = (f32[4,7,7,128]{3,0,2,1:T(4,128)}, f32[4,7,7,128]{3,0,2,1:T(4,128)}, f32[4,7,7,128]{3,0,2,1:T(4,128)}) fusion(f32[4,7,7,128]{3,0,2,1:T(4,128)S(1)} %copy-done, f32[4,7,7,128]{3,0,2,1:T(4,128)} %bitcast.7, f32[4,7,7,128]{3,0,2,1:T(4,128)S(1)} %copy-done.1, f32[4,7,7,128]{3,0,2,1:T(4,128)} %param.9), kind=kLoop, calls=%fused_computation.2 | loop fusion | flops 301056 | bytes 702464 | tf_op jit(solution)/shard_map/sub | solution.py:399
  51.3 0.0 copy-done.2
  51.3 0.6 %copy.10 = bf16[16,16,128]{2,1,0:T(8,128)(2,1)} copy(bf16[16,16,128]{2,1,0:T(8,128)(2,1)S(1)} %copy-done.2) | data formatting | bytes 131072
Async XLA Ops:
  0.6 48.9 %copy-start = (f32[4,7,7,128]{3,0,2,1:T(4,128)S(1)}, f32[4,7,7,128]{3,0,2,1:T(4,128)}, u32[]{:S(2)}) copy-start(f32[4,7,7,128]{3,0,2,1:T(4,128)} %param.7) | copy-start | bytes 301060
  0.6 48.9 %copy-start.1 = (f32[4,7,7,128]{3,0,2,1:T(4,128)S(1)}, f32[4,7,7,128]{3,0,2,1:T(4,128)}, u32[]{:S(2)}) copy-start(f32[4,7,7,128]{3,0,2,1:T(4,128)} %param.8) | copy-start | bytes 301060
  49.5 1.8 %copy-start.2 = (bf16[16,16,128]{2,1,0:T(8,128)(2,1)S(1)}, bf16[16,16,128]{2,1,0:T(8,128)(2,1)}, u32[]{:S(2)}) copy-start(bf16[16,16,128]{2,1,0:T(8,128)(2,1)} %get-tuple-element.15) | copy-start | bytes 196612

commit v5 on v4

--- a/solution.py
+++ b/solution.py
@@ -328,17 +328,17 @@
     def b_hop(way, s, c):
         step = side(way)
         rows = pl.ds(8 * c, 8)
-        alone = s == 2 or c == chunk(way, 1)
-        src = bk_out.at[rows, tile_cols(col_at(step * s))] if alone else bk_sum.at[way]
+        alone = s == 2 or way == 1 or c == 1
+        src = bk_out.at[rows, tile_cols(col_at(step * s))] if alone else bk_sum
         sem = (way * 2 + s - 1) * 2 + c
-        return remote(src, bk_got.at[way, s - 1, rows], b_send.at[sem], b_recv.at[sem], {"col": col_at(step)})
-
-    def b_step(way):
-        c = chunk(way, 0)
-        b_hop(way, 2, c).wait_recv()
-        own = bk_out[8 * c : 8 * c + 8, tile_cols(col_at(1 if way == 0 else -1)), :].astype(F32)
-        bk_sum[way] = (own + bk_got[way, 1, 8 * c : 8 * c + 8].astype(F32)).astype(BF16)
-        start(b_hop(way, 1, c))
+        to = col_at(2 if way == 1 and s == 2 else step)
+        return remote(src, bk_got.at[way, s - 1, rows], b_send.at[sem], b_recv.at[sem], {"col": to})
+
+    def b_step():
+        b_hop(0, 2, 0).wait_recv()
+        own = bk_out[0:8, tile_cols(col_at(1)), :].astype(F32)
+        bk_sum[...] = (own + bk_got[0, 1, 0:8].astype(F32)).astype(BF16)
+        start(b_hop(0, 1, 0))
 
     back_part(0)
     start(b_hop(0, 2, 0))
@@ -357,25 +357,29 @@
     back_part(1)
     start(b_hop(1, 2, 1))
     start(b_hop(0, 1, 1))
+    start(b_hop(1, 1, 1))
+    b_step()
     g_relay()
     for way in range(2):
         start(g_hop(way, 2))
-    b_step(0)
-    b_step(1)
     for way in range(2):
         for c in range(2):
             b_hop(way, 1, c).wait_recv()
-
-    def shrink(at, carry):
+    b_hop(1, 2, 1).wait_recv()
+
+    def shrink(far, at, carry):
         u = jnp.where(at < 8, at + 4, jnp.where(at < 12, at - 8, at))
         back = bk_out[at, tile_cols(q)].astype(F32)
         for way in range(2):
             back = back + bk_got[way, 0, at].astype(F32)
+        if far:
+            back = back + bk_got[1, 1, at].astype(F32)
         moved = x_buf[u, tile_cols(q)].astype(F32) - 0.05 * back
         out_codes[u] = (moved - jnp.clip(moved, -0.02, 0.02)).astype(BF16)
         return carry
 
-    lax.fori_loop(0, 16, shrink, 0)
+    lax.fori_loop(0, 8, functools.partial(shrink, False), 0)
+    lax.fori_loop(8, 16, functools.partial(shrink, True), 0)
 
     for way in range(2):
         for kind in (2, 3):
@@ -438,7 +442,7 @@
             vmem((2, 4, 32, 896), BF16),
             vmem((512, 896), F32),
             vmem((16, 64, 128), BF16),
-            vmem((2, 8, 16, 128), BF16),
+            vmem((8, 16, 128), BF16),
             vmem((2, 2, 16, 16, 128), BF16),
             dma((3,)),
             dma((8,)), dma((8,)), dma((8,)), dma((8,)), dma((3,)), dma((3,)),

time: 52.1 us -> 51.2 us (0.983)
  Pallas kernels: 48.8 us -> 47.9 us
    pallas_call x1, Pallas kernels: 48.8 us -> 47.9 us  [local(): pl.pallas_call(kernel, out_shape=(jax.ShapeDtypeStruct(codes.shape, BF16)...]
where the time goes in v5:
time: 51.2 us; the launch traced here: 51 us
  Pallas kernels  47.9 us (94%)
  other arithmetic  1.8 us (4%)
  between operations  0.68 us (1%)
  local copies, waits for them, and re-layouts  0.64 us (1%)
    pallas_call x1, Pallas kernels, local(): pl.pallas_call(kernel, out_shape=(jax.ShapeDtypeStruct(codes.shape, BF16)...  47.9 us
    sub x1, other arithmetic, adam_update(): master - 0.05 * (new_moment / first_fix) / (jnp.sqrt(new_second / second_...  1.8 us

profile of v5, /device:TPU:1, one launch (start us, length us, event | category | flops | bytes accessed | tf_op | source)
XLA Modules:
  0.0 51.0 jit_solution(15394315778854161546)
XLA Ops:
  0.6 0.0 copy-start
  0.6 0.0 copy-start.1
  0.7 47.9 %dictionary_step.1 = (bf16[16,16,128]{2,1,0:T(8,128)(2,1)}, f32[49,4,128]{2,1,0:T(4,128)}) custom-call(bf16[16,16,128]{2,1,0:T(8,128)(2,1)} %codes.1, bf16[16,16,128]{2,1,0:T(8,128)(2,1)} %image.1, f32[49,4,128]{2,1,0:T(4,128)} %bitcast.6), custom_call_target="tpu_custom_call" | custom-call | tf_op jit(solution)/shard_map/dictionary_step/pallas_call | solution.py:416
  48.5 0.0 copy-done
  48.5 0.0 copy-done.1
  48.5 0.0 copy-start.2
  48.6 1.8 %divide_subtract_fusion = (f32[4,7,7,128]{3,0,2,1:T(4,128)}, f32[4,7,7,128]{3,0,2,1:T(4,128)}, f32[4,7,7,128]{3,0,2,1:T(4,128)}) fusion(f32[4,7,7,128]{3,0,2,1:T(4,128)S(1)} %copy-done, f32[4,7,7,128]{3,0,2,1:T(4,128)} %bitcast.7, f32[4,7,7,128]{3,0,2,1:T(4,128)S(1)} %copy-done.1, f32[4,7,7,128]{3,0,2,1:T(4,128)} %param.9), kind=kLoop, calls=%fused_computation.2 | loop fusion | flops 301056 | bytes 702464 | tf_op jit(solution)/shard_map/sub | solution.py:403
  50.4 0.0 copy-done.2
  50.4 0.6 %copy.10 = bf16[16,16,128]{2,1,0:T(8,128)(2,1)} copy(bf16[16,16,128]{2,1,0:T(8,128)(2,1)S(1)} %copy-done.2) | data formatting | bytes 131072
Async XLA Ops:
  0.6 47.9 %copy-start = (f32[4,7,7,128]{3,0,2,1:T(4,128)S(1)}, f32[4,7,7,128]{3,0,2,1:T(4,128)}, u32[]{:S(2)}) copy-start(f32[4,7,7,128]{3,0,2,1:T(4,128)} %param.7) | copy-start | bytes 301060
  0.6 47.9 %copy-start.1 = (f32[4,7,7,128]{3,0,2,1:T(4,128)S(1)}, f32[4,7,7,128]{3,0,2,1:T(4,128)}, u32[]{:S(2)}) copy-start(f32[4,7,7,128]{3,0,2,1:T(4,128)} %param.8) | copy-start | bytes 301060
  48.5 1.8 %copy-start.2 = (bf16[16,16,128]{2,1,0:T(8,128)(2,1)S(1)}, bf16[16,16,128]{2,1,0:T(8,128)(2,1)}, u32[]{:S(2)}) copy-start(bf16[16,16,128]{2,1,0:T(8,128)(2,1)} %get-tuple-element.15) | copy-start | bytes 196612

commit v6 on v5

--- a/solution.py
+++ b/solution.py
@@ -358,10 +358,10 @@
     start(b_hop(1, 2, 1))
     start(b_hop(0, 1, 1))
     start(b_hop(1, 1, 1))
+    for way in range(2):
+        start(g_hop(way, 2))
     b_step()
     g_relay()
-    for way in range(2):
-        start(g_hop(way, 2))
     for way in range(2):
         for c in range(2):
             b_hop(way, 1, c).wait_recv()

time: 51.2 us -> 51.2 us (level)
  no operation moved by 1% of the time
where the time goes in v6:
time: 51.2 us; the launch traced here: 51 us
  Pallas kernels  47.9 us (94%)
  other arithmetic  1.8 us (4%)
  between operations  0.68 us (1%)
  local copies, waits for them, and re-layouts  0.64 us (1%)
    pallas_call x1, Pallas kernels, local(): pl.pallas_call(kernel, out_shape=(jax.ShapeDtypeStruct(codes.shape, BF16)...  47.9 us
    sub x1, other arithmetic, adam_update(): master - 0.05 * (new_moment / first_fix) / (jnp.sqrt(new_second / second_...  1.8 us

profile of v6, /device:TPU:1, one launch (start us, length us, event | category | flops | bytes accessed | tf_op | source)
XLA Modules:
  0.0 51.0 jit_solution(8950408283398343606)
XLA Ops:
  0.6 0.0 copy-start
  0.6 0.0 copy-start.1
  0.7 47.9 %dictionary_step.1 = (bf16[16,16,128]{2,1,0:T(8,128)(2,1)}, f32[49,4,128]{2,1,0:T(4,128)}) custom-call(bf16[16,16,128]{2,1,0:T(8,128)(2,1)} %codes.1, bf16[16,16,128]{2,1,0:T(8,128)(2,1)} %image.1, f32[49,4,128]{2,1,0:T(4,128)} %bitcast.6), custom_call_target="tpu_custom_call" | custom-call | tf_op jit(solution)/shard_map/dictionary_step/pallas_call | solution.py:416
  48.5 0.0 copy-done
  48.5 0.0 copy-done.1
  48.5 0.0 copy-start.2
  48.5 1.8 %divide_subtract_fusion = (f32[4,7,7,128]{3,0,2,1:T(4,128)}, f32[4,7,7,128]{3,0,2,1:T(4,128)}, f32[4,7,7,128]{3,0,2,1:T(4,128)}) fusion(f32[4,7,7,128]{3,0,2,1:T(4,128)S(1)} %copy-done, f32[4,7,7,128]{3,0,2,1:T(4,128)} %bitcast.7, f32[4,7,7,128]{3,0,2,1:T(4,128)S(1)} %copy-done.1, f32[4,7,7,128]{3,0,2,1:T(4,128)} %param.9), kind=kLoop, calls=%fused_computation.2 | loop fusion | flops 301056 | bytes 702464 | tf_op jit(solution)/shard_map/sub | solution.py:403
  50.3 0.0 copy-done.2
  50.3 0.6 %copy.10 = bf16[16,16,128]{2,1,0:T(8,128)(2,1)} copy(bf16[16,16,128]{2,1,0:T(8,128)(2,1)S(1)} %copy-done.2) | data formatting | bytes 131072
Async XLA Ops:
  0.6 47.9 %copy-start = (f32[4,7,7,128]{3,0,2,1:T(4,128)S(1)}, f32[4,7,7,128]{3,0,2,1:T(4,128)}, u32[]{:S(2)}) copy-start(f32[4,7,7,128]{3,0,2,1:T(4,128)} %param.7) | copy-start | bytes 301060
  0.6 47.9 %copy-start.1 = (f32[4,7,7,128]{3,0,2,1:T(4,128)S(1)}, f32[4,7,7,128]{3,0,2,1:T(4,128)}, u32[]{:S(2)}) copy-start(f32[4,7,7,128]{3,0,2,1:T(4,128)} %param.8) | copy-start | bytes 301060
  48.5 1.8 %copy-start.2 = (bf16[16,16,128]{2,1,0:T(8,128)(2,1)S(1)}, bf16[16,16,128]{2,1,0:T(8,128)(2,1)}, u32[]{:S(2)}) copy-start(bf16[16,16,128]{2,1,0:T(8,128)(2,1)} %get-tuple-element.15) | copy-start | bytes 196612
